TPU v7x, 512 devices: a whole 4x4x16 slice. The times are simulated.
512 devices in a mesh: gz: 32 (over x, z_lo, core), gy: 16 (over z_hi, y).
Axes of the slice: x: 4, y: 4, z: 16 (z_hi: 4, z_lo: 4; z = z_hi * 4 + z_lo), core: 2. Of those that a mesh axis runs over, the one named last changes fastest.
Arguments:
- features: bfloat16 [32, 128, 128, 256], P(None, 'gz', 'gy'), may hold values from -6 to 6
- scale_first: float32 [32], replicated, may hold values from 0.5 to 2
- shift_first: float32 [32], replicated, may hold values from -3 to 3
- conv_first: bfloat16 [3, 3, 32, 32], replicated, may hold values from -0.375 to 0.375
- bias_first: float32 [32], replicated, may hold values from -3 to 3
- scale_second: float32 [32], replicated, may hold values from 0.5 to 2
- shift_second: float32 [32], replicated, may hold values from -3 to 3
- conv_second: bfloat16 [3, 3, 32, 32], replicated, may hold values from -0.375 to 0.375
- bias_second: float32 [32], replicated, may hold values from -3 to 3
- flow_weight: bfloat16 [2, 32], replicated, may hold values from -1 to 1
Outputs:
- smoothed: float32 [3, 128, 128, 256], P(None, 'gz', 'gy')
All inputs are finite; a program needn't handle non-finite values.
Results may differ from a plain program's by a relative error of at most 0.0015.
Values may be sent and summed in bfloat16 or wider, within the bound.
A program may use at most 64 MiB of HBM per device.

v0:
```python
import jax
import jax.numpy as jnp
from jax import lax
from jax.sharding import PartitionSpec as P


def extended(value, sides, width):
    for axis, dim in sides:
        devices, length = (lax.axis_size(axis), value.shape[dim])
        up = [(i, (i + 1) % devices) for i in range(devices - 1)]
        down = [(j, i) for i, j in up]
        last = lax.slice_in_dim(value, length - width, length, axis=dim)
        first = lax.slice_in_dim(value, 0, width, axis=dim)
        before = lax.ppermute(last, axis, up)
        after = lax.ppermute(first, axis, down)
        value = jnp.concatenate([before, value, after], axis=dim)
    return value


def shift_cols(source, delta):
    if delta == 0:
        return source
    zeros = jnp.zeros(source.shape[:-1] + (1,), source.dtype)
    if delta == 1:
        return jnp.concatenate([source[..., 1:], zeros], -1)
    return jnp.concatenate([zeros, source[..., :-1]], -1)


def plane_conv(source, weight, plane_axes, count_z, count_y, start_z, start_y):
    summed = None
    for row_tap in range(3):
        for col_tap in range(3):
            offset = {1: 0, 2: 0, 3: 0}
            offset[plane_axes[0]] = row_tap - 1
            offset[plane_axes[1]] = col_tap - 1
            low_z = start_z + offset[1]
            low_y = start_y + offset[2]
            window = lax.slice(
                source,
                (0, low_z, low_y, 0),
                (source.shape[0], low_z + count_z, low_y + count_y, source.shape[3]),
            )
            window = shift_cols(window, offset[3])
            term = jnp.einsum(
                "oc,czyx->ozyx",
                weight[row_tap, col_tap],
                window,
                preferred_element_type=jnp.float32,
            )
            summed = term if summed is None else summed + term
    return summed


def column(vector):
    return vector[:, None, None, None]


def inside_mask(low_z, count_z, low_y, count_y, total_z, total_y):
    place_z = low_z + jnp.arange(count_z, dtype=jnp.int32)
    place_y = low_y + jnp.arange(count_y, dtype=jnp.int32)
    inside_z = (place_z >= 0) & (place_z < total_z)
    inside_y = (place_y >= 0) & (place_y < total_y)
    return inside_z[None, :, None, None] & inside_y[None, None, :, None]


def shards(
    features,
    scale_first,
    shift_first,
    conv_first,
    bias_first,
    scale_second,
    shift_second,
    conv_second,
    bias_second,
    flow_weight,
):
    depth, rows = (features.shape[1], features.shape[2])
    first_z = lax.axis_index("gz") * depth
    first_y = lax.axis_index("gy") * rows
    total_z = depth * lax.axis_size("gz")
    total_y = rows * lax.axis_size("gy")
    flows = []
    unit = jax.nn.relu(
        features.astype(jnp.float32) * column(scale_first) + column(shift_first)
    ).astype(jnp.bfloat16)
    padded = extended(unit, (("gz", 1), ("gy", 2)), 2)
    for plane_axes in ((2, 3), (1, 3), (1, 2)):
        grow_z = 1 if 1 in plane_axes else 0
        grow_y = 1 if 2 in plane_axes else 0
        hidden = plane_conv(
            padded,
            conv_first,
            plane_axes,
            depth + 2 * grow_z,
            rows + 2 * grow_y,
            2 - grow_z,
            2 - grow_y,
        ) + column(bias_first)
        active = jax.nn.relu(hidden * column(scale_second) + column(shift_second))
        active = jnp.where(
            inside_mask(
                first_z - grow_z,
                depth + 2 * grow_z,
                first_y - grow_y,
                rows + 2 * grow_y,
                total_z,
                total_y,
            ),
            active,
            0.0,
        ).astype(jnp.bfloat16)
        output = plane_conv(active, conv_second, plane_axes, depth, rows, grow_z, grow_y)
        block = (output + column(bias_second) + features.astype(jnp.float32)).astype(jnp.bfloat16)
        flows.append(
            jnp.einsum("kc,czyx->kzyx", flow_weight, block, preferred_element_type=jnp.float32)
        )
    flow_xy, flow_xz, flow_yz = flows
    mean_flow = jnp.stack(
        [
            0.5 * (flow_xz[0] + flow_yz[0]),
            0.5 * (flow_xy[0] + flow_yz[1]),
            0.5 * (flow_xy[1] + flow_xz[1]),
        ]
    )
    ext = extended(mean_flow, (("gz", 1), ("gy", 2)), 1)
    ext = 0.25 * ext[:, :-2] + 0.5 * ext[:, 1:-1] + 0.25 * ext[:, 2:]
    ext = 0.25 * ext[:, :, :-2] + 0.5 * ext[:, :, 1:-1] + 0.25 * ext[:, :, 2:]
    return 0.25 * shift_cols(ext, -1) + 0.5 * ext + 0.25 * shift_cols(ext, 1)


def solution(mesh):
    return jax.shard_map(
        shards,
        mesh=mesh,
        in_specs=(P(None, "gz", "gy", None), P(), P(), P(), P(), P(), P(), P(), P(), P()),
        out_specs=P(None, "gz", "gy", None),
        check_vma=False,
    )
```

profile of v0, /device:TPU:154, one launch (start us, length us, event | category | flops | bytes accessed | tf_op | source)
XLA Modules:
  0.0 103.8 jit_solution(3829591521907324500)
XLA Ops:
  0.0 1.4 %fusion.28 = bf16[32,4,8,256]{3,0,2,1:T(8,128)(2,1)S(1)} fusion(f32[32]{0:T(128)} %param.12, f32[32]{0:T(128)} %param.11, bf16[32,4,8,256]{3,2,1,0:T(8,128)(2,1)} %param.10), kind=kLoop, calls=%fused_computation.71 | loop fusion | flops 1310720 | bytes 1048832 | tf_op jit(solution)/shard_map/convert_element_type | solution.py:86
  1.5 1.9 %collective-permute-start = (bf16[32,2,8,256]{3,0,2,1:T(8,128)(2,1)S(1)}, bf16[32,2,8,256]{3,0,2,1:T(8,128)(2,1)S(1)}, u32[]{:S(2)}, u32[]{:S(2)}) collective-permute-start(bf16[32,2,8,256]{3,0,2,1:T(8,128)(2,1)S(1)} %get-tuple-element.35), channel_id=1, source_target_pairs={{0,16},{16,32},{32,48},{48,64},{64,80},{80,96},{96,112},{112,128},... | collective-permute-start | bytes 786440 | tf_op jit(solution)/shard_map/ppermute | solution.py:14
  3.4 6.3 %collective-permute-start.1 = (bf16[32,2,8,256]{3,0,2,1:T(8,128)(2,1)S(1)}, bf16[32,2,8,256]{3,0,2,1:T(8,128)(2,1)S(1)}, u32[]{:S(2)}, u32[]{:S(2)}) collective-permute-start(bf16[32,2,8,256]{3,0,2,1:T(8,128)(2,1)S(1)} %get-tuple-element.36), channel_id=1, source_target_pairs={{16,0},{32,16},{48,32},{64,48},{80,64},{96,80},{112,96},{128,112},... | collective-permute-start | bytes 786440 | tf_op jit(solution)/shard_map/ppermute | solution.py:15
  9.8 0.7 broadcast_and_fusion.2
  10.5 0.6 broadcast_and_fusion
  11.2 0.8 collective-permute-done
  12.0 1.7 %collective-permute-done.1 = bf16[32,2,8,256]{3,0,2,1:T(8,128)(2,1)S(1)} collective-permute-done((bf16[32,2,8,256]{3,0,2,1:T(8,128)(2,1)S(1)}, bf16[32,2,8,256]{3,0,2,1:T(8,128)(2,1)S(1)}, u32[]{:S(2)}, u32[]{:S(2)}) %collective-permute-start.1) | collective-permute-done | bytes 262176 | tf_op jit(solution)/shard_map/ppermute | solution.py:15
  13.8 0.8 fusion.285
  15.0 8.8 %collective-permute-start.2 = (bf16[32,8,2,256]{3,0,2,1:T(8,128)(2,1)}, bf16[32,8,2,256]{3,0,2,1:T(8,128)(2,1)S(1)}, u32[]{:S(2)}, u32[]{:S(2)}) collective-permute-start(bf16[32,8,2,256]{3,0,2,1:T(8,128)(2,1)} %get-tuple-element.13), channel_id=1, source_target_pairs={{0,1},{1,2},{2,3},{3,4},{4,5},{5,6},{6,7},{7,8},{8,9},{9,10},{10,1... | collective-permute-start | bytes 786440 | tf_op jit(solution)/shard_map/ppermute | solution.py:14
  23.8 1.9 %collective-permute-start.3 = (bf16[32,8,2,256]{3,0,2,1:T(8,128)(2,1)}, bf16[32,8,2,256]{3,0,2,1:T(8,128)(2,1)}, u32[]{:S(2)}, u32[]{:S(2)}) collective-permute-start(bf16[32,8,2,256]{3,0,2,1:T(8,128)(2,1)} %get-tuple-element.14), channel_id=1, source_target_pairs={{1,0},{2,1},{3,2},{4,3},{5,4},{6,5},{7,6},{8,7},{9,8},{10,9},{11,1... | collective-permute-start | bytes 786440 | tf_op jit(solution)/shard_map/ppermute | solution.py:15
  26.1 0.8 fusion.54
  29.9 0.9 fusion.64
  30.9 0.7 fusion.287
  34.3 0.7 copy-done.1
  35.0 1.3 %fusion.23 = f32[2,4,8,256]{3,0,2,1:T(2,128)S(1)} fusion(f32[4,8,256,32]{2,3,1,0:T(8,128)S(1)} %convolution_add_fusion.21, f32[32]{0:T(128)} %param.18, bf16[32,4,8,255]{3,0,2,1:T(8,128)(2,1)S(1)} %get-tuple-element.17, bf16[32,4,8,256]{3,2,1,0:T(8,128)(2,1)S(1)} %copy-done.1, bf16[3,3,32,32]{3,2,1,0:T(8,128)(2,1)} %param.17, bf16[2,32]{1,0:T(2,128)(2,1)S(1)} %copy-done), kind=kOutput, calls=%fused_computation.66 | convolution fusion | flops 19136512 | bytes 2169472 | tf_op jit(solution)/shard_map/kc,czyx->kzyx/dot_general | solution.py:116
  36.4 9.4 %collective-permute-done.2 = bf16[32,8,2,256]{3,0,2,1:T(8,128)(2,1)S(1)} collective-permute-done((bf16[32,8,2,256]{3,0,2,1:T(8,128)(2,1)}, bf16[32,8,2,256]{3,0,2,1:T(8,128)(2,1)S(1)}, u32[]{:S(2)}, u32[]{:S(2)}) %collective-permute-start.2) | collective-permute-done | bytes 262176 | tf_op jit(solution)/shard_map/ppermute | solution.py:14
  45.8 11.9 %collective-permute-done.3 = bf16[32,8,2,256]{3,0,2,1:T(8,128)(2,1)} collective-permute-done((bf16[32,8,2,256]{3,0,2,1:T(8,128)(2,1)}, bf16[32,8,2,256]{3,0,2,1:T(8,128)(2,1)}, u32[]{:S(2)}, u32[]{:S(2)}) %collective-permute-start.3) | collective-permute-done | bytes 262176 | tf_op jit(solution)/shard_map/ppermute | solution.py:15
  57.7 1.2 %pad_maximum_fusion = bf16[32,8,12,256]{3,0,2,1:T(8,128)(2,1)S(1)} fusion(bf16[32,8,2,256]{3,0,2,1:T(8,128)(2,1)} %collective-permute-done.3, bf16[32,2,8,256]{3,0,2,1:T(8,128)(2,1)S(1)} %collective-permute-done.1, bf16[32,4,8,256]{3,0,2,1:T(8,128)(2,1)S(1)} %fusion.28, bf16[32,2,8,256]{3,0,2,1:T(8,128)(2,1)S(1)} %collective-permute-done, ...), kind=kLoop, calls=%fused_computation.5 | loop fusion | flops 3145728 | bytes 3145728 | tf_op jit(solution)/shard_map/concatenate | solution.py:16
  59.5 1.5 %maximum_maximum_fusion = (bf16[32,8,10,256]{3,0,2,1:T(8,128)(2,1)S(1)}, bf16[32,8,10,256]{3,0,2,1:T(8,128)(2,1)S(1)}) fusion(bf16[32,2,8,256]{3,0,2,1:T(8,128)(2,1)S(1)} %collective-permute-done.1, bf16[32,4,8,256]{3,0,2,1:T(8,128)(2,1)S(1)} %fusion.28, bf16[32,2,8,256]{3,0,2,1:T(8,128)(2,1)S(1)} %collective-permute-done, ...), kind=kLoop, calls=%fused_computation.51 | loop fusion | flops 3932160 | bytes 4194304 | tf_op jit(solution)/shard_map/concatenate | solution.py:16
  61.8 0.7 fusion.283
  68.2 0.7 fusion.288
  72.0 1.2 %fusion.33 = bf16[32,6,10,256]{3,0,2,1:T(8,128)(2,1)S(1)} fusion(bf16[32,8,10,256]{3,0,2,1:T(8,128)(2,1)S(1)} %get-tuple-element.12, f32[6,10,256,32]{2,3,1,0:T(8,128)S(1)} %fusion.36, f32[6,10,256,32]{2,3,1,0:T(8,128)S(1)} %fusion.38, f32[6,10,256,32]{2,3,1,0:T(8,128)S(1)} %fusion.40, f32[6,10,256,32]{2,3,1,0:T(8,128)S(1)} %fusion.42, ...), kind=kOutput, calls=%fused_computation.75 | convolution fusion | flops 38338560 | bytes 17705472 | tf_op jit(solution)/shard_map/oc,czyx->ozyx/dot_general | solution.py:44
  75.1 1.3 %convolution_add_fusion.13 = f32[4,8,256,32]{2,3,1,0:T(8,128)} fusion(f32[4,8,256,32]{2,3,1,0:T(8,128)S(1)} %convolution_add_fusion.14, bf16[32,6,10,256]{3,0,2,1:T(8,128)(2,1)S(1)} %fusion.33, bf16[3,3,32,32]{3,2,1,0:T(8,128)(2,1)S(1)} %copy-done.4), kind=kOutput, calls=%fused_computation.33 | convolution fusion | flops 17039360 | bytes 2629632 | tf_op jit(solution)/shard_map/oc,czyx->ozyx/dot_general | solution.py:44
  76.4 1.9 %fusion.24 = f32[2,4,8,256]{3,0,2,1:T(2,128)S(1)} fusion(f32[4,8,256,32]{2,3,1,0:T(8,128)} %convolution_add_fusion.13, bf16[32,6,10,256]{3,0,2,1:T(8,128)(2,1)S(1)} %fusion.33, f32[32]{0:T(128)S(1)} %copy-done.10, bf16[32,4,8,256]{3,2,1,0:T(8,128)(2,1)S(1)} %copy-done.1, bf16[3,3,32,32]{3,2,1,0:T(8,128)(2,1)S(1)} %copy-done.4, bf16[2,32]{1,0:T(2,128)(2,1)S(1)} %copy-done), kind=kOutput, calls=%fused_computation.67 | convolution fusion | flops 19136512 | bytes 2171904 | tf_op jit(solution)/shard_map/kc,czyx->kzyx/dot_general | solution.py:116
  78.2 0.7 fusion.25
  79.1 2.0 %collective-permute-start.4 = (f32[3,1,8,256]{3,0,2,1:T(4,128)S(1)}, f32[3,1,8,256]{3,0,2,1:T(4,128)S(1)}, u32[]{:S(2)}, u32[]{:S(2)}) collective-permute-start(f32[3,1,8,256]{3,0,2,1:T(4,128)S(1)} %get-tuple-element.41), channel_id=1, source_target_pairs={{0,16},{16,32},{32,48},{48,64},{64,80},{80,96},{96,112},{112,128},... | collective-permute-start | bytes 73736 | tf_op jit(solution)/shard_map/ppermute | solution.py:14
  81.1 6.3 %collective-permute-start.5 = (f32[3,1,8,256]{3,0,2,1:T(4,128)S(1)}, f32[3,1,8,256]{3,0,2,1:T(4,128)S(1)}, u32[]{:S(2)}, u32[]{:S(2)}) collective-permute-start(f32[3,1,8,256]{3,0,2,1:T(4,128)S(1)} %get-tuple-element.42), channel_id=1, source_target_pairs={{16,0},{32,16},{48,32},{64,48},{80,64},{96,80},{112,96},{128,112},... | collective-permute-start | bytes 73736 | tf_op jit(solution)/shard_map/ppermute | solution.py:15
  87.4 1.6 %collective-permute-done.5 = f32[3,1,8,256]{3,0,2,1:T(4,128)S(1)} collective-permute-done((f32[3,1,8,256]{3,0,2,1:T(4,128)S(1)}, f32[3,1,8,256]{3,0,2,1:T(4,128)S(1)}, u32[]{:S(2)}, u32[]{:S(2)}) %collective-permute-start.5) | collective-permute-done | bytes 24608 | tf_op jit(solution)/shard_map/ppermute | solution.py:15
  89.0 1.9 %collective-permute-start.6 = (f32[3,6,1,256]{3,0,2,1:T(4,128)S(1)}, f32[3,6,1,256]{3,0,2,1:T(4,128)S(1)}, u32[]{:S(2)}, u32[]{:S(2)}) collective-permute-start(f32[3,6,1,256]{3,0,2,1:T(4,128)S(1)} %get-tuple-element.37), channel_id=1, source_target_pairs={{0,1},{1,2},{2,3},{3,4},{4,5},{5,6},{6,7},{7,8},{8,9},{9,10},{10,1... | collective-permute-start | bytes 55304 | tf_op jit(solution)/shard_map/ppermute | solution.py:14
  90.9 3.9 %collective-permute-start.7 = (f32[3,6,1,256]{3,0,2,1:T(4,128)S(1)}, f32[3,6,1,256]{3,0,2,1:T(4,128)S(1)}, u32[]{:S(2)}, u32[]{:S(2)}) collective-permute-start(f32[3,6,1,256]{3,0,2,1:T(4,128)S(1)} %get-tuple-element.38), channel_id=1, source_target_pairs={{1,0},{2,1},{3,2},{4,3},{5,4},{6,5},{7,6},{8,7},{9,8},{10,9},{11,1... | collective-permute-start | bytes 55304 | tf_op jit(solution)/shard_map/ppermute | solution.py:15
  94.8 7.8 %collective-permute-done.7 = f32[3,6,1,256]{3,0,2,1:T(4,128)S(1)} collective-permute-done((f32[3,6,1,256]{3,0,2,1:T(4,128)S(1)}, f32[3,6,1,256]{3,0,2,1:T(4,128)S(1)}, u32[]{:S(2)}, u32[]{:S(2)}) %collective-permute-start.7) | collective-permute-done | bytes 18464 | tf_op jit(solution)/shard_map/ppermute | solution.py:15
  103.2 0.7 copy.12
  (92 shorter events, 19.2 us)
Async XLA Ops:
  0.0 34.3 %copy-start = (bf16[2,32]{1,0:T(2,128)(2,1)S(1)}, bf16[2,32]{1,0:T(2,128)(2,1)}, u32[]{:S(2)}) copy-start(bf16[2,32]{1,0:T(2,128)(2,1)} %param.19) | copy-start | bytes 388
  1.5 10.5 %collective-permute-start = (bf16[32,2,8,256]{3,0,2,1:T(8,128)(2,1)S(1)}, bf16[32,2,8,256]{3,0,2,1:T(8,128)(2,1)S(1)}, u32[]{:S(2)}, u32[]{:S(2)}) collective-permute-start(bf16[32,2,8,256]{3,0,2,1:T(8,128)(2,1)S(1)} %get-tuple-element.35), channel_id=1, source_target_pairs={{0,16},{16,32},{32,48},{48,64},{64,80},{80,96},{96,112},{112,128},... | collective-permute-start | bytes 786440 | tf_op jit(solution)/shard_map/ppermute | solution.py:14
  3.4 10.2 %collective-permute-start.1 = (bf16[32,2,8,256]{3,0,2,1:T(8,128)(2,1)S(1)}, bf16[32,2,8,256]{3,0,2,1:T(8,128)(2,1)S(1)}, u32[]{:S(2)}, u32[]{:S(2)}) collective-permute-start(bf16[32,2,8,256]{3,0,2,1:T(8,128)(2,1)S(1)} %get-tuple-element.36), channel_id=1, source_target_pairs={{16,0},{32,16},{48,32},{64,48},{80,64},{96,80},{112,96},{128,112},... | collective-permute-start | bytes 786440 | tf_op jit(solution)/shard_map/ppermute | solution.py:15
  14.6 11.1 %copy-start.2 = (bf16[3,3,32,32]{3,2,1,0:T(8,128)(2,1)S(1)}, bf16[3,3,32,32]{3,2,1,0:T(8,128)(2,1)}, u32[]{:S(2)}) copy-start(bf16[3,3,32,32]{3,2,1,0:T(8,128)(2,1)} %param.13) | copy-start | bytes 55300
  15.0 30.8 %collective-permute-start.2 = (bf16[32,8,2,256]{3,0,2,1:T(8,128)(2,1)}, bf16[32,8,2,256]{3,0,2,1:T(8,128)(2,1)S(1)}, u32[]{:S(2)}, u32[]{:S(2)}) collective-permute-start(bf16[32,8,2,256]{3,0,2,1:T(8,128)(2,1)} %get-tuple-element.13), channel_id=1, source_target_pairs={{0,1},{1,2},{2,3},{3,4},{4,5},{5,6},{6,7},{7,8},{8,9},{9,10},{10,1... | collective-permute-start | bytes 786440 | tf_op jit(solution)/shard_map/ppermute | solution.py:14
  23.8 33.9 %collective-permute-start.3 = (bf16[32,8,2,256]{3,0,2,1:T(8,128)(2,1)}, bf16[32,8,2,256]{3,0,2,1:T(8,128)(2,1)}, u32[]{:S(2)}, u32[]{:S(2)}) collective-permute-start(bf16[32,8,2,256]{3,0,2,1:T(8,128)(2,1)} %get-tuple-element.14), channel_id=1, source_target_pairs={{1,0},{2,1},{3,2},{4,3},{5,4},{6,5},{7,6},{8,7},{9,8},{10,9},{11,1... | collective-permute-start | bytes 786440 | tf_op jit(solution)/shard_map/ppermute | solution.py:15
  29.2 0.7 copy-start.5
  29.2 0.7 copy-start.6
  29.2 0.7 copy-start.8
  30.9 0.9 copy-start.3
  34.0 1.0 %copy-start.1 = (bf16[32,4,8,256]{3,2,1,0:T(8,128)(2,1)S(1)}, bf16[32,4,8,256]{3,2,1,0:T(8,128)(2,1)}, u32[]{:S(2)}) copy-start(bf16[32,4,8,256]{3,2,1,0:T(8,128)(2,1)} %param.10) | copy-start | bytes 1572868
  66.9 0.7 copy-start.7
  67.0 0.7 copy-start.9
  67.0 0.7 copy-start.12
  68.2 0.9 copy-start.4
  71.3 0.7 copy-start.11
  75.1 1.3 %copy-start.10 = (f32[32]{0:T(128)S(1)}, f32[32]{0:T(128)}, u32[]{:S(2)}) copy-start(f32[32]{0:T(128)} %param.18) | copy-start | bytes 388
  79.1 8.3 %collective-permute-start.4 = (f32[3,1,8,256]{3,0,2,1:T(4,128)S(1)}, f32[3,1,8,256]{3,0,2,1:T(4,128)S(1)}, u32[]{:S(2)}, u32[]{:S(2)}) collective-permute-start(f32[3,1,8,256]{3,0,2,1:T(4,128)S(1)} %get-tuple-element.41), channel_id=1, source_target_pairs={{0,16},{16,32},{32,48},{48,64},{64,80},{80,96},{96,112},{112,128},... | collective-permute-start | bytes 73736 | tf_op jit(solution)/shard_map/ppermute | solution.py:14
  81.1 7.9 %collective-permute-start.5 = (f32[3,1,8,256]{3,0,2,1:T(4,128)S(1)}, f32[3,1,8,256]{3,0,2,1:T(4,128)S(1)}, u32[]{:S(2)}, u32[]{:S(2)}) collective-permute-start(f32[3,1,8,256]{3,0,2,1:T(4,128)S(1)} %get-tuple-element.42), channel_id=1, source_target_pairs={{16,0},{32,16},{48,32},{64,48},{80,64},{96,80},{112,96},{128,112},... | collective-permute-start | bytes 73736 | tf_op jit(solution)/shard_map/ppermute | solution.py:15
  89.0 5.9 %collective-permute-start.6 = (f32[3,6,1,256]{3,0,2,1:T(4,128)S(1)}, f32[3,6,1,256]{3,0,2,1:T(4,128)S(1)}, u32[]{:S(2)}, u32[]{:S(2)}) collective-permute-start(f32[3,6,1,256]{3,0,2,1:T(4,128)S(1)} %get-tuple-element.37), channel_id=1, source_target_pairs={{0,1},{1,2},{2,3},{3,4},{4,5},{5,6},{6,7},{7,8},{8,9},{9,10},{10,1... | collective-permute-start | bytes 55304 | tf_op jit(solution)/shard_map/ppermute | solution.py:14
  90.9 11.7 %collective-permute-start.7 = (f32[3,6,1,256]{3,0,2,1:T(4,128)S(1)}, f32[3,6,1,256]{3,0,2,1:T(4,128)S(1)}, u32[]{:S(2)}, u32[]{:S(2)}) collective-permute-start(f32[3,6,1,256]{3,0,2,1:T(4,128)S(1)} %get-tuple-element.38), channel_id=1, source_target_pairs={{1,0},{2,1},{3,2},{4,3},{5,4},{6,5},{7,6},{8,7},{9,8},{10,9},{11,1... | collective-permute-start | bytes 55304 | tf_op jit(solution)/shard_map/ppermute | solution.py:15
where the time goes:
time: 104 us
  waiting for transfers between devices  33.2 us (32%)
  starting transfers between devices  33 us (32%)
  matrix products  23.6 us (23%)
  other arithmetic  7.02 us (7%)
  local copies, waits for them, and re-layouts  6.32 us (6%)
    ppermute x4, waiting for transfers between devices, extended(): after = lax.ppermute(first, axis, down)  22.9 us
    dot_general x51, matrix products, plane_conv(): jnp.einsum('oc,czyx->ozyx', weight[row_tap, col_tap], window, preferred_e...  19.7 us
    ppermute x4, starting transfers between devices, extended(): after = lax.ppermute(first, axis, down)  18.5 us
    ppermute x4, starting transfers between devices, extended(): before = lax.ppermute(last, axis, up)  14.6 us
    ppermute x4, waiting for transfers between devices, extended(): before = lax.ppermute(last, axis, up)  10.2 us
    dot_general x3, matrix products, shards(): jnp.einsum('kc,czyx->kzyx', flow_weight, block, preferred_element_type=jn...  3.87 us
    concatenate x5, other arithmetic, extended(): value = jnp.concatenate([before, value, after], axis=dim)  3.74 us
  transfers between devices with their start and end apart: 8, of which 6 were waited for; matrix products, arithmetic and copies ran while one was open for 10% of the time, Pallas kernels for 0%

commit v1 on v0

v1 whole, which is shorter than its diff:
```python
import jax
import jax.numpy as jnp
from jax import lax
from jax.experimental import pallas as pl
from jax.experimental.pallas import tpu as pltpu
from jax.sharding import PartitionSpec as P

MESH = pl.DeviceIdType.MESH
F32 = jnp.float32
BF16 = jnp.bfloat16
C = 32
Z = 4
Y = 8
X = 256
R = C * Y


def iota(shape, dim):
    return lax.broadcasted_iota(jnp.int32, shape, dim)


def dot(a, b):
    return jnp.dot(a, b, preferred_element_type=F32)


def one_hot(flags):
    return jnp.where(flags, 1.0, 0.0).astype(BF16)


def from_left(value):
    moved = pltpu.roll(value, 1, axis=1)
    return jnp.where(iota(value.shape, 1) == 0, 0.0, moved)


def from_right(value):
    last = value.shape[1] - 1
    moved = pltpu.roll(value, last, axis=1)
    return jnp.where(iota(value.shape, 1) == last, 0.0, moved)


def kernel(
    x_hbm, s1_hbm, t1_hbm, w1_hbm, b1_hbm, s2_hbm, t2_hbm, w2_hbm, b2_hbm, fw_hbm,
    out,
    xin, par, w1, w2, fw, raw, ux, edge, ez, halo,
    cols, wxy, wxz, wyz, whx, why, bxy, bxz, byz, fres, hid, acc, sm,
    rz, ys, yr,
    lsem, ssem, rsem,
):
    gz, gy = lax.axis_index("gz"), lax.axis_index("gy")
    nz, ny = lax.axis_size("gz"), lax.axis_size("gy")
    has_z = (gz > 0, gz < nz - 1)
    has_y = (gy > 0, gy < ny - 1)
    z_of = (gz - 1, gz + 1)
    y_of = (gy - 1, gy + 1)

    barrier = pltpu.get_barrier_semaphore()
    for side in range(2):
        @pl.when(has_z[side])
        def _():
            pl.semaphore_signal(barrier, inc=1, device_id=(z_of[side], gy), device_id_type=MESH)

        @pl.when(has_y[side])
        def _():
            pl.semaphore_signal(barrier, inc=1, device_id=(gz, y_of[side]), device_id_type=MESH)

    order = (0, 3, 1, 2)
    loads = {z: pltpu.make_async_copy(x_hbm.at[:, z], xin.at[:, z], lsem.at[z]) for z in order}
    params = [
        pltpu.make_async_copy(source, par.at[i], lsem.at[Z + i])
        for i, source in enumerate((s1_hbm, t1_hbm, b1_hbm, s2_hbm, t2_hbm, b2_hbm))
    ]
    weights = [
        pltpu.make_async_copy(source, target, lsem.at[Z + 6 + i])
        for i, (source, target) in enumerate(((w1_hbm, w1), (w2_hbm, w2), (fw_hbm, fw)))
    ]
    for copy in (*params, loads[0], loads[3], loads[1], loads[2], *weights):
        copy.start()

    for side in range(2):
        slot = (0, Z + 1)[side]

        @pl.when(jnp.logical_not(has_z[side]))
        def _():
            ux[slot, 1] = jnp.zeros((R, X), BF16)
            halo[slot] = jnp.zeros((2, C, X), BF16)

        @pl.when(jnp.logical_not(has_y[side]))
        def _():
            for ze in range(1, Z + 1):
                halo[ze, side] = jnp.zeros((C, X), BF16)

        for yside in range(2):
            @pl.when(has_z[side] & jnp.logical_not(has_y[yside]))
            def _():
                halo[slot, yside] = jnp.zeros((C, X), BF16)

    for copy in params:
        copy.wait()
    pick = iota((R, C), 0) // Y == iota((R, C), 1)

    def column(row):
        return jnp.sum(jnp.where(pick, row, 0.0), axis=1, keepdims=True)

    b1_row, s2_row, t2_row, b2_row = par[2], par[3], par[4], par[5]
    cols[0] = jnp.broadcast_to(column(par[0]), (R, 128))
    cols[1] = jnp.broadcast_to(column(par[1]), (R, 128))
    cols[2] = jnp.broadcast_to(column(s2_row), (R, 128))
    cols[3] = jnp.broadcast_to(column(b1_row * s2_row + t2_row), (R, 128))

    def wide(i):
        half = cols[i]
        return jnp.concatenate([half, half], axis=1)

    rows, lanes = iota((2 * C, R), 0), iota((2 * C, R), 1)
    edge_pick = one_hot(lanes == (rows % C) * Y + (rows // C) * (Y - 1))
    for z in order:
        loads[z].wait()
        value = xin[:, z].astype(F32).reshape(R, X)
        raw[z] = value.astype(BF16)
        unit = jnp.maximum(value * wide(0) + wide(1), 0.0).astype(BF16)
        ux[z + 1, 1] = unit
        edge[z] = dot(edge_pick, unit).astype(BF16).reshape(2, C, X)

    def remote(source, target, i, zi, yi):
        return pltpu.make_async_remote_copy(
            src_ref=source, dst_ref=target, send_sem=ssem.at[i], recv_sem=rsem.at[i],
            device_id=(zi, yi), device_id_type=MESH,
        )

    send_ez = [remote(edge.at[(0, Z - 1)[s]], ez.at[1 - s], s, z_of[s], gy) for s in range(2)]
    send_slab = [
        remote(ux.at[(1, Z)[s], 1], ux.at[(Z + 1, 0)[s], 1], 2 + s, z_of[s], gy) for s in range(2)
    ]
    send_y = [
        remote(edge.at[:, s], halo.at[pl.ds(1, Z), 1 - s], 4 + s, gz, y_of[s]) for s in range(2)
    ]
    send_corner = [
        [
            remote(ez.at[zs, ys_], halo.at[(0, Z + 1)[zs], 1 - ys_], 6 + 2 * zs + ys_, gz, y_of[ys_])
            for ys_ in range(2)
        ]
        for zs in range(2)
    ]

    peers = sum(flag.astype(jnp.int32) for flag in (*has_z, *has_y))
    pl.semaphore_wait(barrier, peers)

    for side in range(2):
        @pl.when(has_z[side])
        def _():
            send_ez[side].start()
    for side in range(2):
        @pl.when(has_y[side])
        def _():
            send_y[side].start()
    for side in range(2):
        @pl.when(has_z[side])
        def _():
            send_slab[side].start()

    for copy in weights:
        copy.wait()
    spread = one_hot(iota((C, R), 1) // Y == iota((C, R), 0))
    repeat = one_hot(pick)
    wide_w1 = dot(w1[...].reshape(9 * C, C), spread).astype(BF16)
    shift = iota((R, R), 1) % Y - iota((R, R), 0) % Y
    for j in range(3):
        banded = None
        for i in range(3):
            k = 3 * i + j
            full = dot(repeat, wide_w1[k * C : (k + 1) * C])
            term = jnp.where(shift == i - 1, full, 0.0)
            banded = term if banded is None else banded + term
            wxz[i, :, j * R : (j + 1) * R] = jnp.where(shift == 0, full, 0.0).astype(BF16)
        wxy[:, j * R : (j + 1) * R] = banded.astype(BF16)
    for i in range(3):
        banded = None
        for j in range(3):
            k = 3 * i + j
            full = dot(repeat, wide_w1[k * C : (k + 1) * C])
            term = jnp.where(shift == j - 1, full, 0.0)
            banded = term if banded is None else banded + term
        wyz[i] = banded.astype(BF16)
    reach = 6 * C
    rows, lanes = iota((R, reach), 0) % Y, (iota((R, reach), 1) // C) % 2
    touched = ((rows == 0) & (lanes == 0)) | ((rows == Y - 1) & (lanes == 1))
    packed_x = jnp.zeros((C, reach), F32)
    packed_y = jnp.zeros((C, reach), F32)
    for tap in range(3):
        for side in range(2):
            put = one_hot(iota((C, reach), 1) == iota((C, reach), 0) + (2 * tap + side) * C)
            packed_x += dot(w1[2 * side, tap], put)
            packed_y += dot(w1[tap, 2 * side], put)
    whx[...] = jnp.where(touched, dot(repeat, packed_x.astype(BF16)), 0.0).astype(BF16)
    why[...] = jnp.where(touched, dot(repeat, packed_y.astype(BF16)), 0.0).astype(BF16)

    lanes16 = iota((16, R), 1) % Y
    rows16 = iota((16, R), 0)
    fw16 = jnp.where(
        iota((16, C), 0) < Y, jnp.broadcast_to(fw[0:1, :].astype(F32), (16, C)),
        jnp.broadcast_to(fw[1:2, :].astype(F32), (16, C)),
    )
    fres[...] = jnp.where(rows16 % Y == lanes16, dot(fw16.astype(BF16), spread), 0.0).astype(BF16)
    bias = jnp.sum(fw16 * b2_row, axis=1, keepdims=True)
    for k in range(2):
        fw_k = jnp.broadcast_to(fw[k : k + 1, :].astype(F32), (16, C)).astype(BF16)
        taps = {}
        for i in range(3):
            for j in range(3):
                g = dot(fw_k, w2[i, j])
                high = g.astype(BF16)
                low = (g - high.astype(F32)).astype(BF16)
                taps[i, j] = (dot(high, spread), dot(low, spread))
        for part in range(2):
            for a in range(3):
                band_xy = jnp.zeros((16, R), F32)
                band_yz = jnp.zeros((16, R), F32)
                for b in range(3):
                    hit = rows16 == (lanes16 + (17 - b)) % 16
                    band_xy += jnp.where(hit, taps[b, a][part], 0.0)
                    band_yz += jnp.where(hit, taps[a, b][part], 0.0)
                at = ((part * 3 + a) * 2 + k) * 16
                bxy[at : at + 16, :] = band_xy.astype(BF16)
                byz[at : at + 16, :] = band_yz.astype(BF16)
        for i in range(3):
            for j in range(3):
                for part in range(2):
                    at = ((part * 9 + i * 3 + j) * 2) * Y
                    keep = (rows16 // Y == k) & (rows16 % Y == lanes16)
                    value = jnp.where(keep, taps[i, j][part], 0.0)
                    if k == 0:
                        bxz[at : at + 16, :] = value.astype(BF16)
                    else:
                        bxz[at : at + 16, :] = (bxz[at : at + 16, :].astype(F32) + value).astype(BF16)

    def shifted(ze):
        value = ux[ze, 1].astype(F32)
        ux[ze, 0] = from_left(value).astype(BF16)
        ux[ze, 2] = from_right(value).astype(BF16)

    for ze in range(1, Z + 1):
        shifted(ze)

    for side in range(2):
        @pl.when(has_z[side])
        def _():
            send_ez[side].wait_send()
            send_ez[1 - side].wait_recv()
            for yside in range(2):
                @pl.when(has_y[yside])
                def _():
                    send_corner[side][yside].start()

    acc[...] = jnp.zeros_like(acc)
    for z in range(Z):
        hid[0, z] = dot(wxy[...], ux[z + 1].reshape(3 * R, X))
        xz = dot(wxz[1], ux[z + 1].reshape(3 * R, X))
        yz = dot(wyz[1], ux[z + 1, 1])
        for i in (0, 2):
            if 1 <= z + i <= Z:
                xz += dot(wxz[i], ux[z + i].reshape(3 * R, X))
                yz += dot(wyz[i], ux[z + i, 1])
        hid[1, z] = xz
        hid[2, z] = yz
        residual = dot(fres[...], raw[z]) + bias
        r0, r1 = residual[:Y], residual[Y:]
        acc[1, z + 1, 0, 0] = 2.0 * r0
        acc[1, z + 1, 1, 0] = r0 + r1
        acc[1, z + 1, 2, 0] = 2.0 * r1

    for side in range(2):
        @pl.when(has_z[side])
        def _():
            send_slab[1 - side].wait_recv()
    for ze in (0, Z + 1):
        shifted(ze)
    for z, i in ((0, 0), (Z - 1, 2)):
        hid[1, z] += dot(wxz[i], ux[z + i].reshape(3 * R, X))
        hid[2, z] += dot(wyz[i], ux[z + i, 1])

    def active(plane, z):
        return jnp.maximum(hid[plane, z] * wide(2) + wide(3), 0.0).astype(BF16)

    for z in range(Z):
        both = dot(bxz[...], active(1, z))
        part = both[:144] + both[144:]
        for i in range(3):
            for j in range(3):
                at = (i * 3 + j) * 16
                acc[j, z + 2 - i, 0, 0] += part[at : at + Y]
                acc[j, z + 2 - i, 2, 0] += part[at + Y : at + 16]

    for side in range(2):
        @pl.when(has_y[side])
        def _():
            send_y[1 - side].wait_recv()
            for zside in range(2):
                @pl.when(has_z[zside])
                def _():
                    send_corner[zside][1 - side].wait_recv()
    for z in range(Z):
        beside = halo[z + 1].reshape(2 * C, X)
        wider = beside.astype(F32)
        three = jnp.concatenate([from_left(wider).astype(BF16), beside, from_right(wider).astype(BF16)], axis=0)
        hid[0, z] += dot(whx[...], three)
        hid[2, z] += dot(why[...], halo[z : z + 3].reshape(6 * C, X))
        both = dot(bxy[...], active(0, z))
        part = (both[:96] + both[96:]).reshape(3, 2, 2, Y, X)
        for j in range(3):
            acc[j, z + 1, 1] += part[j, 0]
            acc[j, z + 1, 2] += part[j, 1]
        both = dot(byz[...], active(2, z))
        part = (both[:96] + both[96:]).reshape(3, 2, 2, Y, X)
        for i in range(3):
            acc[1, z + 2 - i, 0] += part[i, 0]
            acc[1, z + 2 - i, 1] += part[i, 1]

    rows16x = iota((16, X), 0)
    outside = ((rows16x == 15) & jnp.logical_not(has_y[0])) | ((rows16x == Y) & jnp.logical_not(has_y[1]))
    flow = {}
    for ze in range(Z + 2):
        for comp in range(3):
            value = (
                from_left(acc[0, ze, comp].reshape(16, X))
                + acc[1, ze, comp].reshape(16, X)
                + from_right(acc[2, ze, comp].reshape(16, X))
            )
            value = jnp.where(outside, 0.0, value)
            if ze == 0:
                value = jnp.where(has_z[0], value, 0.0)
            if ze == Z + 1:
                value = jnp.where(has_z[1], value, 0.0)
            value = 0.125 * (from_left(value) + from_right(value)) + 0.25 * value
            flow[ze, comp] = 0.5 * value + 0.25 * (pltpu.roll(value, 1, axis=0) + pltpu.roll(value, 15, axis=0))
    for comp in range(3):
        for zs in range(Z + 4):
            value = None
            for ze, weight in ((zs - 2, 0.25), (zs - 1, 0.5), (zs, 0.25)):
                if 0 <= ze < Z + 2:
                    term = weight * flow[ze, comp]
                    value = term if value is None else value + term
            sm[0, zs, comp] = value[:Y]
            sm[1, zs, comp] = value[Y:]

    send_rz = [
        [
            remote(sm.at[t, pl.ds((0, Z + 2)[s], 2)], rz.at[1 - s, t], 10 + 2 * t + s, z_of[s], gy)
            for s in range(2)
        ]
        for t in range(2)
    ]
    send_ry = [remote(ys.at[s], yr.at[1 - s], 14 + s, gz, y_of[s]) for s in range(2)]
    for t in (1, 0):
        for side in range(2):
            @pl.when(has_z[side])
            def _():
                send_rz[t][side].start()
    for side in range(2):
        @pl.when(jnp.logical_not(has_z[side]))
        def _():
            rz[side] = jnp.zeros((2, 2, 3, Y, X), F32)

        @pl.when(jnp.logical_not(has_y[side]))
        def _():
            yr[side] = jnp.zeros((3, Y, X), F32)

    for side in range(2):
        @pl.when(has_z[side])
        def _():
            send_rz[1][1 - side].wait_recv()
    row = iota((Y, X), 0)
    for comp in range(3):
        up, down = None, None
        for z in range(Z):
            value = sm[1, z + 2, comp] + rz[z // 2, 1, z % 2, comp]
            high = jnp.where(row < 2, value, 0.0)
            low = jnp.where(row >= Y - 2, value, 0.0)
            if z:
                high = pltpu.roll(high, 2 * z, axis=0)
            if z < Z - 1:
                low = pltpu.roll(low, 2 * z + 2, axis=0)
            up = high if up is None else up + high
            down = low if down is None else down + low
        ys[1, comp] = up
        ys[0, comp] = down
    for side in range(2):
        @pl.when(has_y[side])
        def _():
            send_ry[side].start()
    for side in range(2):
        @pl.when(has_z[side])
        def _():
            send_rz[0][1 - side].wait_recv()
    for comp in range(3):
        for z in range(Z):
            sm[0, z + 2, comp] += rz[z // 2, 0, z % 2, comp]
    for side in range(2):
        @pl.when(has_y[side])
        def _():
            send_ry[1 - side].wait_recv()
    for comp in range(3):
        for z in range(Z):
            first = yr[0, comp]
            if z:
                first = pltpu.roll(first, Y - 2 * z, axis=0)
            last = yr[1, comp]
            if z < Z - 1:
                last = pltpu.roll(last, Y - 2 - 2 * z, axis=0)
            beyond = jnp.where(row < 2, first, jnp.where(row >= Y - 2, last, 0.0))
            out[comp, z] = sm[0, z + 2, comp] + beyond

    for side in range(2):
        @pl.when(has_z[side])
        def _():
            send_slab[side].wait_send()
            send_rz[0][side].wait_send()
            send_rz[1][side].wait_send()

        @pl.when(has_y[side])
        def _():
            send_y[side].wait_send()
            send_ry[side].wait_send()
            for zside in range(2):
                @pl.when(has_z[zside])
                def _():
                    send_corner[zside][side].wait_send()


def block(features, s1, t1, w1, b1, s2, t2, w2, b2, fw):
    def row(v):
        return v.reshape(1, C)

    vm = pltpu.VMEM
    dma = pltpu.SemaphoreType.DMA
    return pl.pallas_call(
        kernel,
        out_shape=jax.ShapeDtypeStruct((3, Z, Y, X), F32),
        in_specs=[pl.BlockSpec(memory_space=pl.ANY)] * 10,
        out_specs=pl.BlockSpec(memory_space=pltpu.VMEM),
        scratch_shapes=[
            vm((C, Z, Y, X), BF16),
            vm((6, 1, C), F32),
            vm((3, 3, C, C), BF16),
            vm((3, 3, C, C), BF16),
            vm((2, C), BF16),
            vm((Z, R, X), BF16),
            vm((Z + 2, 3, R, X), BF16),
            vm((Z, 2, C, X), BF16),
            vm((2, 2, C, X), BF16),
            vm((Z + 2, 2, C, X), BF16),
            vm((4, R, 128), F32),
            vm((R, 3 * R), BF16),
            vm((3, R, 3 * R), BF16),
            vm((3, R, R), BF16),
            vm((R, 6 * C), BF16),
            vm((R, 6 * C), BF16),
            vm((192, R), BF16),
            vm((288, R), BF16),
            vm((192, R), BF16),
            vm((16, R), BF16),
            vm((3, Z, R, X), F32),
            vm((3, Z + 2, 3, 2, Y, X), F32),
            vm((2, Z + 4, 3, Y, X), F32),
            vm((2, 2, 2, 3, Y, X), F32),
            vm((2, 3, Y, X), F32),
            vm((2, 3, Y, X), F32),
            dma((Z + 9,)),
            dma((16,)),
            dma((16,)),
        ],
        compiler_params=pltpu.CompilerParams(
            collective_id=0, has_side_effects=True, vmem_limit_bytes=48 * 1024 * 1024
        ),
    )(features, row(s1), row(t1), w1, row(b1), row(s2), row(t2), w2, row(b2), fw)


def solution(mesh):
    return jax.shard_map(
        block,
        mesh=mesh,
        in_specs=(P(None, "gz", "gy", None), P(), P(), P(), P(), P(), P(), P(), P(), P()),
        out_specs=P(None, "gz", "gy", None),
        check_vma=False,
    )
```

time: 104 us -> 37.7 us (0.36)
  the two profiles are of different devices: /device:TPU:154 before, /device:TPU:249 now
where the time goes in v1:
time: 37.7 us; the launch traced here: 37.5 us
  Pallas kernels  33.3 us (88%)
  local copies, waits for them, and re-layouts  4.16 us (11%)
    pallas_call x1, Pallas kernels, block(): pl.pallas_call(kernel, out_shape=jax.ShapeDtypeStruct((3, Z, Y, X), F32),...  33.3 us
    unnamed x21, local copies, waits for them, and re-layouts  4.16 us

profile of v1, /device:TPU:249, one launch (start us, length us, event | category | flops | bytes accessed | tf_op | source)
XLA Modules:
  0.0 37.5 jit_solution(16663472951544665807)
XLA Ops:
  0.0 0.0 copy-start.6
  0.0 0.0 copy-start.7
  0.0 0.0 copy-start.8
  0.0 0.0 copy-start.9
  0.0 0.0 copy-start.3
  0.0 0.0 copy-start.4
  0.0 0.0 copy-start.5
  0.0 0.6 %copy-done.6 = f32[32]{0:T(128)S(1)} copy-done((f32[32]{0:T(128)S(1)}, f32[32]{0:T(128)}, u32[]{:S(2)}) %copy-start.6) | copy-done | bytes 152
  0.7 0.0 copy-done.7
  0.7 0.0 copy-done.8
  0.7 0.0 copy-done.9
  0.7 0.0 copy-done.3
  0.7 0.0 copy-done.4
  0.7 0.0 copy-done.5
  0.8 0.0 copy-start
  0.8 1.0 %copy-done = bf16[32,4,8,256]{3,2,1,0:T(8,128)(2,1)S(1)} copy-done((bf16[32,4,8,256]{3,2,1,0:T(8,128)(2,1)S(1)}, bf16[32,4,8,256]{3,2,1,0:T(8,128)(2,1)}, u32[]{:S(2)}) %copy-start) | copy-done | bytes 524312
  1.8 0.0 copy-start.1
  1.8 0.9 %copy-done.1 = bf16[3,3,32,32]{3,2,1,0:T(8,128)(2,1)S(1)} copy-done((bf16[3,3,32,32]{3,2,1,0:T(8,128)(2,1)S(1)}, bf16[3,3,32,32]{3,2,1,0:T(8,128)(2,1)}, u32[]{:S(2)}) %copy-start.1) | copy-done | bytes 18456
  2.7 0.0 copy-start.2
  2.7 0.9 %copy-done.2 = bf16[3,3,32,32]{3,2,1,0:T(8,128)(2,1)S(1)} copy-done((bf16[3,3,32,32]{3,2,1,0:T(8,128)(2,1)S(1)}, bf16[3,3,32,32]{3,2,1,0:T(8,128)(2,1)}, u32[]{:S(2)}) %copy-start.2) | copy-done | bytes 18456
  3.6 33.3 %shard_map.100 = f32[3,4,8,256]{3,2,1,0:T(8,128)S(1)} custom-call(bf16[32,4,8,256]{3,2,1,0:T(8,128)(2,1)S(1)} %copy-done, f32[1,32]{1,0:T(1,128)S(1)} %bitcast.6, f32[1,32]{1,0:T(1,128)S(1)} %bitcast.7, bf16[3,3,32,32]{3,2,1,0:T(8,128)(2,1)S(1)} %copy-done.1, f32[1,32]{1,0:T(1,128)S(1)} %bitcast.8, f32[1,32]{1,0:T(1,128)S(1)} %bitcast.9, ...), custom_call_target="tpu_custom_call" | custom-call | tf_op jit(solution)/shard_map/pallas_call | solution.py:435
  36.8 0.6 %copy.12 = f32[3,4,8,256]{3,2,1,0:T(8,128)} copy(f32[3,4,8,256]{3,2,1,0:T(8,128)S(1)} %shard_map.100) | data formatting | bytes 196608
Async XLA Ops:
  0.0 0.7 %copy-start.6 = (f32[32]{0:T(128)S(1)}, f32[32]{0:T(128)}, u32[]{:S(2)}) copy-start(f32[32]{0:T(128)} %param.15) | copy-start | bytes 388
  0.0 0.7 %copy-start.7 = (f32[32]{0:T(128)S(1)}, f32[32]{0:T(128)}, u32[]{:S(2)}) copy-start(f32[32]{0:T(128)} %param.16) | copy-start | bytes 388
  0.0 0.7 %copy-start.8 = (f32[32]{0:T(128)S(1)}, f32[32]{0:T(128)}, u32[]{:S(2)}) copy-start(f32[32]{0:T(128)} %param.18) | copy-start | bytes 388
  0.0 0.7 %copy-start.9 = (bf16[2,32]{1,0:T(2,128)(2,1)S(1)}, bf16[2,32]{1,0:T(2,128)(2,1)}, u32[]{:S(2)}) copy-start(bf16[2,32]{1,0:T(2,128)(2,1)} %fw_hbm.1) | copy-start | bytes 388
  0.0 0.7 %copy-start.3 = (f32[32]{0:T(128)S(1)}, f32[32]{0:T(128)}, u32[]{:S(2)}) copy-start(f32[32]{0:T(128)} %param.11) | copy-start | bytes 388
  0.0 0.7 %copy-start.4 = (f32[32]{0:T(128)S(1)}, f32[32]{0:T(128)}, u32[]{:S(2)}) copy-start(f32[32]{0:T(128)} %param.12) | copy-start | bytes 388
  0.0 0.7 %copy-start.5 = (f32[32]{0:T(128)S(1)}, f32[32]{0:T(128)}, u32[]{:S(2)}) copy-start(f32[32]{0:T(128)} %param.14) | copy-start | bytes 388
  0.8 1.0 %copy-start = (bf16[32,4,8,256]{3,2,1,0:T(8,128)(2,1)S(1)}, bf16[32,4,8,256]{3,2,1,0:T(8,128)(2,1)}, u32[]{:S(2)}) copy-start(bf16[32,4,8,256]{3,2,1,0:T(8,128)(2,1)} %x_hbm.1) | copy-start | bytes 1572868
  1.8 0.9 %copy-start.1 = (bf16[3,3,32,32]{3,2,1,0:T(8,128)(2,1)S(1)}, bf16[3,3,32,32]{3,2,1,0:T(8,128)(2,1)}, u32[]{:S(2)}) copy-start(bf16[3,3,32,32]{3,2,1,0:T(8,128)(2,1)} %w1_hbm.1) | copy-start | bytes 55300
  2.7 0.9 %copy-start.2 = (bf16[3,3,32,32]{3,2,1,0:T(8,128)(2,1)S(1)}, bf16[3,3,32,32]{3,2,1,0:T(8,128)(2,1)}, u32[]{:S(2)}) copy-start(bf16[3,3,32,32]{3,2,1,0:T(8,128)(2,1)} %w2_hbm.1) | copy-start | bytes 55300

commit v2 on v1

v2 whole, which is shorter than its diff:
```python
import jax
import jax.numpy as jnp
from jax import lax
from jax.experimental import pallas as pl
from jax.experimental.pallas import tpu as pltpu
from jax.sharding import PartitionSpec as P

MESH = pl.DeviceIdType.MESH
F32 = jnp.float32
BF16 = jnp.bfloat16
C = 32
Z = 4
Y = 8
X = 256
R = C * Y


def iota(shape, dim):
    return lax.broadcasted_iota(jnp.int32, shape, dim)


def dot(a, b):
    return jnp.dot(a, b, preferred_element_type=F32)


def one_hot(flags):
    return jnp.where(flags, 1.0, 0.0).astype(BF16)


def from_left(value):
    moved = pltpu.roll(value, 1, axis=1)
    return jnp.where(iota(value.shape, 1) == 0, 0.0, moved)


def from_right(value):
    last = value.shape[1] - 1
    moved = pltpu.roll(value, last, axis=1)
    return jnp.where(iota(value.shape, 1) == last, 0.0, moved)


def kernel(
    x_hbm, s1_hbm, t1_hbm, w1_hbm, b1_hbm, s2_hbm, t2_hbm, w2_hbm, b2_hbm, fw_hbm,
    out,
    xin, par, w1, w2, fw, raw, ux, edge, ez, halo,
    cols, cols_e, wxy, wxz, wyz, wxy_e, wyz_e, whx, why, bxy, bxz, byz, bxy_e, byz_e, fres,
    hid, hid_e, acc, sm,
    rz, ys, yr, ds, dr,
    lsem, ssem, rsem,
):
    gz, gy = lax.axis_index("gz"), lax.axis_index("gy")
    nz, ny = lax.axis_size("gz"), lax.axis_size("gy")
    has_z = (gz > 0, gz < nz - 1)
    has_y = (gy > 0, gy < ny - 1)
    z_of = (gz - 1, gz + 1)
    y_of = (gy - 1, gy + 1)

    barrier = pltpu.get_barrier_semaphore()
    for side in range(2):
        @pl.when(has_z[side])
        def _():
            pl.semaphore_signal(barrier, inc=1, device_id=(z_of[side], gy), device_id_type=MESH)

        @pl.when(has_y[side])
        def _():
            pl.semaphore_signal(barrier, inc=1, device_id=(gz, y_of[side]), device_id_type=MESH)

    order = (0, 3, 1, 2)
    loads = {z: pltpu.make_async_copy(x_hbm.at[:, z], xin.at[:, z], lsem.at[z]) for z in order}
    params = [
        pltpu.make_async_copy(source, par.at[i], lsem.at[Z + i])
        for i, source in enumerate((s1_hbm, t1_hbm, b1_hbm, s2_hbm, t2_hbm, b2_hbm))
    ]
    weights = [
        pltpu.make_async_copy(source, target, lsem.at[Z + 6 + i])
        for i, (source, target) in enumerate(((w1_hbm, w1), (w2_hbm, w2), (fw_hbm, fw)))
    ]
    for copy in (*params, loads[0], loads[3], loads[1], loads[2], *weights):
        copy.start()

    for side in range(2):
        slot = (0, Z + 1)[side]

        @pl.when(jnp.logical_not(has_z[side]))
        def _():
            ux[slot, 1] = jnp.zeros((R, X), BF16)
            halo[slot] = jnp.zeros((2, C, X), BF16)

        @pl.when(jnp.logical_not(has_y[side]))
        def _():
            for ze in range(1, Z + 1):
                halo[ze, side] = jnp.zeros((C, X), BF16)

        for yside in range(2):
            @pl.when(has_z[side] & jnp.logical_not(has_y[yside]))
            def _():
                halo[slot, yside] = jnp.zeros((C, X), BF16)

    for copy in params:
        copy.wait()
    pick = iota((R, C), 0) // Y == iota((R, C), 1)

    def column(row):
        return jnp.sum(jnp.where(pick, row, 0.0), axis=1, keepdims=True)

    b1_row, s2_row, t2_row, b2_row = par[2], par[3], par[4], par[5]
    cols[0] = jnp.broadcast_to(column(par[0]), (R, 128))
    cols[1] = jnp.broadcast_to(column(par[1]), (R, 128))
    cols[2] = jnp.broadcast_to(column(s2_row), (R, 128))
    cols[3] = jnp.broadcast_to(column(b1_row * s2_row + t2_row), (R, 128))

    pick_e = iota((2 * C, C), 0) % C == iota((2 * C, C), 1)
    cols_e[0] = jnp.broadcast_to(
        jnp.sum(jnp.where(pick_e, s2_row, 0.0), axis=1, keepdims=True), (2 * C, 128)
    )
    cols_e[1] = jnp.broadcast_to(
        jnp.sum(jnp.where(pick_e, b1_row * s2_row + t2_row, 0.0), axis=1, keepdims=True), (2 * C, 128)
    )

    def wide(half):
        return jnp.concatenate([half, half], axis=1)

    rows, lanes = iota((2 * C, R), 0), iota((2 * C, R), 1)
    edge_pick = one_hot(lanes == (rows % C) * Y + (rows // C) * (Y - 1))
    for z in order:
        loads[z].wait()
        value = xin[:, z].astype(F32).reshape(R, X)
        raw[z] = value.astype(BF16)
        unit = jnp.maximum(value * wide(cols[0]) + wide(cols[1]), 0.0).astype(BF16)
        ux[z + 1, 1] = unit
        edge[z] = dot(edge_pick, unit).astype(BF16).reshape(2, C, X)

    def remote(source, target, i, zi, yi):
        return pltpu.make_async_remote_copy(
            src_ref=source, dst_ref=target, send_sem=ssem.at[i], recv_sem=rsem.at[i],
            device_id=(zi, yi), device_id_type=MESH,
        )

    send_ez = [remote(edge.at[(0, Z - 1)[s]], ez.at[1 - s], s, z_of[s], gy) for s in range(2)]
    send_slab = [
        remote(ux.at[(1, Z)[s], 1], ux.at[(Z + 1, 0)[s], 1], 2 + s, z_of[s], gy) for s in range(2)
    ]
    send_y = [
        remote(edge.at[:, s], halo.at[pl.ds(1, Z), 1 - s], 4 + s, gz, y_of[s]) for s in range(2)
    ]
    send_corner = [
        [
            remote(ez.at[zs, ys_], halo.at[(0, Z + 1)[zs], 1 - ys_], 6 + 2 * zs + ys_, gz, y_of[ys_])
            for ys_ in range(2)
        ]
        for zs in range(2)
    ]

    for copy in weights:
        copy.wait()
    spread = one_hot(iota((C, R), 1) // Y == iota((C, R), 0))
    repeat = one_hot(pick)
    wide_w1 = dot(w1[...].reshape(9 * C, C), spread).astype(BF16)
    shift = iota((R, R), 1) % Y - iota((R, R), 0) % Y
    for j in range(3):
        banded = None
        for i in range(3):
            k = 3 * i + j
            full = dot(repeat, wide_w1[k * C : (k + 1) * C])
            term = jnp.where(shift == i - 1, full, 0.0)
            banded = term if banded is None else banded + term
            wxz[i, :, j * R : (j + 1) * R] = jnp.where(shift == 0, full, 0.0).astype(BF16)
        wxy[:, j * R : (j + 1) * R] = banded.astype(BF16)
    for i in range(3):
        banded = None
        for j in range(3):
            k = 3 * i + j
            full = dot(repeat, wide_w1[k * C : (k + 1) * C])
            term = jnp.where(shift == j - 1, full, 0.0)
            banded = term if banded is None else banded + term
        wyz[i] = banded.astype(BF16)
    for i in range(3):
        wyz_e[i] = dot(edge_pick, wyz[i]).astype(BF16)
    wxy_e[...] = dot(edge_pick, wxy[...]).astype(BF16)
    reach = 6 * C
    touched = iota((2 * C, reach), 0) // C == (iota((2 * C, reach), 1) // C) % 2
    repeat_e = one_hot(pick_e)
    packed_x = jnp.zeros((C, reach), F32)
    packed_y = jnp.zeros((C, reach), F32)
    for tap in range(3):
        for side in range(2):
            put = one_hot(iota((C, reach), 1) == iota((C, reach), 0) + (2 * tap + side) * C)
            packed_x += dot(w1[2 * side, tap], put)
            packed_y += dot(w1[tap, 2 * side], put)
    whx[...] = jnp.where(touched, dot(repeat_e, packed_x.astype(BF16)), 0.0).astype(BF16)
    why[...] = jnp.where(touched, dot(repeat_e, packed_y.astype(BF16)), 0.0).astype(BF16)

    rows, lanes = iota((2 * 16, R), 0) % 16, iota((2 * 16, R), 1) % Y
    first = jnp.broadcast_to(fw[0:1, :].astype(F32), (16, C))
    second = jnp.broadcast_to(fw[1:2, :].astype(F32), (16, C))
    fw32 = jnp.concatenate([first, second], axis=0)
    fw16 = jnp.concatenate([first[:Y], second[:Y]], axis=0)
    highs, lows = [], []
    for i in range(3):
        for j in range(3):
            g = dot(fw32.astype(BF16), w2[i, j])
            high = g.astype(BF16)
            highs.append(high)
            lows.append((g - high.astype(F32)).astype(BF16))
    taps = dot(jnp.concatenate(highs + lows, axis=0), spread).reshape(2, 3, 3, 32, R)
    same = rows == lanes
    for part in range(2):
        for a in range(3):
            band_xy = jnp.zeros((32, R), F32)
            band_yz = jnp.zeros((32, R), F32)
            for b in range(3):
                hit = rows == (lanes + (17 - b)) % 16
                band_xy += jnp.where(hit, taps[part, b, a], 0.0)
                band_yz += jnp.where(hit, taps[part, a, b], 0.0)
            at = (part * 3 + a) * 32
            bxy[at : at + 32, :] = band_xy.astype(BF16)
            byz[at : at + 32, :] = band_yz.astype(BF16)
        for i in range(3):
            for j in range(3):
                value = jnp.where(same, taps[part, i, j], 0.0)
                at = (part * 9 + i * 3 + j) * 16
                bxz[at : at + 16, :] = jnp.concatenate([value[:Y], value[16 : 16 + Y]], axis=0).astype(BF16)
    rows, lanes = iota((R, 2 * C), 0), iota((R, 2 * C), 1)
    edge_put = one_hot(rows == (lanes % C) * Y + (lanes // C) * (Y - 1))
    bxy_e[...] = dot(bxy[...], edge_put).astype(BF16)
    byz_e[...] = dot(byz[...], edge_put).astype(BF16)
    own = iota((16, R), 0) % Y == iota((16, R), 1) % Y
    fres[...] = jnp.where(own, dot(fw16.astype(BF16), spread), 0.0).astype(BF16)
    bias = jnp.sum(fw16 * b2_row, axis=1, keepdims=True)

    peers = sum(flag.astype(jnp.int32) for flag in (*has_z, *has_y))
    pl.semaphore_wait(barrier, peers)

    for side in range(2):
        @pl.when(has_z[side])
        def _():
            send_ez[side].start()
    for side in range(2):
        @pl.when(has_y[side])
        def _():
            send_y[side].start()
    for side in range(2):
        @pl.when(has_z[side])
        def _():
            send_slab[side].start()

    def shifted(ze):
        value = ux[ze, 1].astype(F32)
        ux[ze, 0] = from_left(value).astype(BF16)
        ux[ze, 2] = from_right(value).astype(BF16)

    for ze in range(1, Z + 1):
        shifted(ze)

    row8 = iota((R, X), 0) % Y
    inner = (row8 > 0) & (row8 < Y - 1)

    def active(hidden):
        return jnp.maximum(hidden * wide(cols[2]) + wide(cols[3]), 0.0)

    def active_e(hidden):
        return jnp.maximum(hidden * wide(cols_e[0]) + wide(cols_e[1]), 0.0).astype(BF16)

    def add_xy(z, both):
        part = (both[:96] + both[96:]).reshape(3, 2, 2, Y, X)
        for j in range(3):
            acc[j, z + 1, 1] += part[j, 0]
            acc[j, z + 1, 2] += part[j, 1]

    def add_yz(z, both):
        part = (both[:96] + both[96:]).reshape(3, 2, 2, Y, X)
        for i in range(3):
            acc[1, z + 2 - i, 0] += part[i, 0]
            acc[1, z + 2 - i, 1] += part[i, 1]

    acc[...] = jnp.zeros_like(acc)
    for z in range(Z):
        wide_x = ux[z + 1].reshape(3 * R, X)
        hid_e[0, z] = dot(wxy_e[...], wide_x)
        value = jnp.where(inner, active(dot(wxy[...], wide_x)), 0.0).astype(BF16)
        add_xy(z, dot(bxy[...], value))

    for side in range(2):
        @pl.when(has_z[side])
        def _():
            send_ez[side].wait_send()
            send_ez[1 - side].wait_recv()
            for yside in range(2):
                @pl.when(has_y[yside])
                def _():
                    send_corner[side][yside].start()

    for z in range(Z):
        xz = dot(wxz[1], ux[z + 1].reshape(3 * R, X))
        yz = dot(wyz[1], ux[z + 1, 1])
        yz_e = dot(wyz_e[1], ux[z + 1, 1])
        for i in (0, 2):
            if 1 <= z + i <= Z:
                xz += dot(wxz[i], ux[z + i].reshape(3 * R, X))
                yz += dot(wyz[i], ux[z + i, 1])
                yz_e += dot(wyz_e[i], ux[z + i, 1])
        hid[0, z] = xz
        hid[1, z] = yz
        hid_e[1, z] = yz_e
        residual = dot(fres[...], raw[z]) + bias
        r0, r1 = residual[:Y], residual[Y:]
        acc[1, z + 1, 0, 0] += 2.0 * r0
        acc[1, z + 1, 1, 0] += r0 + r1
        acc[1, z + 1, 2, 0] += 2.0 * r1

    def finish(z):
        both = dot(bxz[...], active(hid[0, z]).astype(BF16))
        part = both[:144] + both[144:]
        for i in range(3):
            for j in range(3):
                at = (i * 3 + j) * 16
                acc[j, z + 2 - i, 0, 0] += part[at : at + Y]
                acc[j, z + 2 - i, 2, 0] += part[at + Y : at + 16]
        add_yz(z, dot(byz[...], jnp.where(inner, active(hid[1, z]), 0.0).astype(BF16)))

    for z in range(1, Z - 1):
        finish(z)

    for side in range(2):
        @pl.when(has_z[side])
        def _():
            send_slab[1 - side].wait_recv()
    for ze in (0, Z + 1):
        shifted(ze)
    for z, i in ((0, 0), (Z - 1, 2)):
        hid[0, z] += dot(wxz[i], ux[z + i].reshape(3 * R, X))
        hid[1, z] += dot(wyz[i], ux[z + i, 1])
        hid_e[1, z] += dot(wyz_e[i], ux[z + i, 1])
        finish(z)

    for side in range(2):
        @pl.when(has_y[side])
        def _():
            send_y[1 - side].wait_recv()
    for z in range(Z):
        beside = halo[z + 1].reshape(2 * C, X)
        wider = beside.astype(F32)
        three = jnp.concatenate([from_left(wider).astype(BF16), beside, from_right(wider).astype(BF16)], axis=0)
        add_xy(z, dot(bxy_e[...], active_e(hid_e[0, z] + dot(whx[...], three))))
    for side in range(2):
        @pl.when(has_y[side])
        def _():
            for zside in range(2):
                @pl.when(has_z[zside])
                def _():
                    send_corner[zside][1 - side].wait_recv()
    for z in range(Z):
        hidden = hid_e[1, z] + dot(why[...], halo[z : z + 3].reshape(6 * C, X))
        add_yz(z, dot(byz_e[...], active_e(hidden)))

    rows16x = iota((16, X), 0)
    outside = ((rows16x == 15) & jnp.logical_not(has_y[0])) | ((rows16x == Y) & jnp.logical_not(has_y[1]))
    flow = {}
    for ze in range(Z + 2):
        for comp in range(3):
            value = (
                from_left(acc[0, ze, comp].reshape(16, X))
                + acc[1, ze, comp].reshape(16, X)
                + from_right(acc[2, ze, comp].reshape(16, X))
            )
            value = jnp.where(outside, 0.0, value)
            if ze == 0:
                value = jnp.where(has_z[0], value, 0.0)
            if ze == Z + 1:
                value = jnp.where(has_z[1], value, 0.0)
            value = 0.125 * (from_left(value) + from_right(value)) + 0.25 * value
            flow[ze, comp] = 0.5 * value + 0.25 * (pltpu.roll(value, 1, axis=0) + pltpu.roll(value, 15, axis=0))
    for comp in range(3):
        for zs in range(Z + 4):
            value = None
            for ze, weight in ((zs - 2, 0.25), (zs - 1, 0.5), (zs, 0.25)):
                if 0 <= ze < Z + 2:
                    term = weight * flow[ze, comp]
                    value = term if value is None else value + term
            sm[0, zs, comp] = value[:Y]
            sm[1, zs, comp] = value[Y:]

    send_rz = [remote(sm.at[0, pl.ds((0, Z + 2)[t], 2)], rz.at[1 - t], 10 + t, z_of[t], gy) for t in range(2)]
    send_ry = [remote(ys.at[s], yr.at[1 - s], 12 + s, gz, y_of[s]) for s in range(2)]
    send_rd = [
        [remote(ds.at[t, s], dr.at[1 - t, 1 - s], 14 + 2 * t + s, z_of[t], y_of[s]) for s in range(2)]
        for t in range(2)
    ]
    row = iota((Y, X), 0)
    sent = (row >= Y - 2, row < 2)

    def moved(value, by):
        return pltpu.roll(value, by % Y, axis=0) if by % Y else value

    for s in range(2):
        for t in range(2):
            for tile in range(2):
                packed = None
                for comp in range(3):
                    for q in range(2):
                        if comp // 2 == tile:
                            value = jnp.where(sent[s], sm[1, (0, Z + 2)[t] + q, comp], 0.0)
                            value = moved(value, (comp % 2) * 4 + 2 * q + (2, 0)[s])
                            packed = value if packed is None else packed + value
                ds[t, s, tile] = packed

            @pl.when(has_z[t] & has_y[s])
            def _():
                send_rd[t][s].start()
    for s in range(2):
        for comp in range(3):
            packed = None
            for z in range(Z):
                value = moved(jnp.where(sent[s], sm[1, z + 2, comp], 0.0), 2 * z + (2, 0)[s])
                packed = value if packed is None else packed + value
            ys[s, comp] = packed

        @pl.when(has_y[s])
        def _():
            send_ry[s].start()
    for t in range(2):
        @pl.when(has_z[t])
        def _():
            send_rz[t].start()

    for side in range(2):
        @pl.when(jnp.logical_not(has_z[side]))
        def _():
            rz[side] = jnp.zeros((2, 3, Y, X), F32)

        @pl.when(jnp.logical_not(has_y[side]))
        def _():
            yr[side] = jnp.zeros((3, Y, X), F32)

        for s in range(2):
            @pl.when(jnp.logical_not(has_z[side] & has_y[s]))
            def _():
                dr[side, s] = jnp.zeros((2, Y, X), F32)

    for side in range(2):
        @pl.when(has_z[side])
        def _():
            send_rz[1 - side].wait_recv()

        @pl.when(has_y[side])
        def _():
            send_ry[1 - side].wait_recv()

        for s in range(2):
            @pl.when(has_z[side] & has_y[s])
            def _():
                send_rd[1 - side][1 - s].wait_recv()
    for comp in range(3):
        for z in range(Z):
            t, q = z // 2, z % 2
            beyond = []
            for s in range(2):
                to = (0, Y - 2)[s]
                value = moved(yr[s, comp], to - 2 * z)
                value += moved(dr[t, s, comp // 2], to - (comp % 2) * 4 - 2 * q)
                beyond.append(value)
            value = jnp.where(row < 2, beyond[0], jnp.where(row >= Y - 2, beyond[1], 0.0))
            out[comp, z] = sm[0, z + 2, comp] + rz[t, q, comp] + value

    for side in range(2):
        @pl.when(has_z[side])
        def _():
            send_slab[side].wait_send()
            send_rz[side].wait_send()

        @pl.when(has_y[side])
        def _():
            send_y[side].wait_send()
            send_ry[side].wait_send()

        for s in range(2):
            @pl.when(has_z[side] & has_y[s])
            def _():
                send_corner[side][s].wait_send()
                send_rd[side][s].wait_send()


def block(features, s1, t1, w1, b1, s2, t2, w2, b2, fw):
    def row(v):
        return v.reshape(1, C)

    vm = pltpu.VMEM
    dma = pltpu.SemaphoreType.DMA
    return pl.pallas_call(
        kernel,
        out_shape=pltpu.VMEM((3, Z, Y, X), F32),
        in_specs=[pl.BlockSpec(memory_space=pltpu.HBM)] * 10,
        out_specs=pl.BlockSpec(memory_space=pltpu.VMEM),
        scratch_shapes=[
            vm((C, Z, Y, X), BF16),
            vm((6, 1, C), F32),
            vm((3, 3, C, C), BF16),
            vm((3, 3, C, C), BF16),
            vm((2, C), BF16),
            vm((Z, R, X), BF16),
            vm((Z + 2, 3, R, X), BF16),
            vm((Z, 2, C, X), BF16),
            vm((2, 2, C, X), BF16),
            vm((Z + 2, 2, C, X), BF16),
            vm((4, R, 128), F32),
            vm((2, 2 * C, 128), F32),
            vm((R, 3 * R), BF16),
            vm((3, R, 3 * R), BF16),
            vm((3, R, R), BF16),
            vm((2 * C, 3 * R), BF16),
            vm((3, 2 * C, R), BF16),
            vm((2 * C, 6 * C), BF16),
            vm((2 * C, 6 * C), BF16),
            vm((192, R), BF16),
            vm((288, R), BF16),
            vm((192, R), BF16),
            vm((192, 2 * C), BF16),
            vm((192, 2 * C), BF16),
            vm((16, R), BF16),
            vm((2, Z, R, X), F32),
            vm((2, Z, 2 * C, X), F32),
            vm((3, Z + 2, 3, 2, Y, X), F32),
            vm((2, Z + 4, 3, Y, X), F32),
            vm((2, 2, 3, Y, X), F32),
            vm((2, 3, Y, X), F32),
            vm((2, 3, Y, X), F32),
            vm((2, 2, 2, Y, X), F32),
            vm((2, 2, 2, Y, X), F32),
            dma((Z + 9,)),
            dma((18,)),
            dma((18,)),
        ],
        compiler_params=pltpu.CompilerParams(
            collective_id=0, has_side_effects=True, vmem_limit_bytes=48 * 1024 * 1024
        ),
    )(*[pltpu.with_memory_space_constraint(v, pltpu.HBM) for v in (features, row(s1), row(t1), w1, row(b1), row(s2), row(t2), w2, row(b2), fw)])


def solution(mesh):
    return jax.shard_map(
        block,
        mesh=mesh,
        in_specs=(P(None, "gz", "gy", None), P(), P(), P(), P(), P(), P(), P(), P(), P()),
        out_specs=P(None, "gz", "gy", None),
        check_vma=False,
    )
```

time: 37.7 us -> 35.7 us (0.947)
  the two profiles are of different devices: /device:TPU:249 before, /device:TPU:158 now
where the time goes in v2:
time: 35.7 us; the launch traced here: 35.6 us
  Pallas kernels  34.9 us (98%)
  local copies, waits for them, and re-layouts  0.64 us (2%)
    pallas_call x1, Pallas kernels, block(): pl.pallas_call(kernel, out_shape=pltpu.VMEM((3, Z, Y, X), F32), in_specs=...  34.9 us

profile of v2, /device:TPU:158, one launch (start us, length us, event | category | flops | bytes accessed | tf_op | source)
XLA Modules:
  0.0 35.6 jit_solution(12238318350926963046)
XLA Ops:
  0.0 34.9 %shard_map.100 = f32[3,4,8,256]{3,2,1,0:T(8,128)S(1)} custom-call(bf16[32,4,8,256]{3,2,1,0:T(8,128)(2,1)} %x_hbm.1, f32[1,32]{1,0:T(1,128)} %bitcast.6, f32[1,32]{1,0:T(1,128)} %bitcast.7, bf16[3,3,32,32]{3,2,1,0:T(8,128)(2,1)} %w1_hbm.1, f32[1,32]{1,0:T(1,128)} %bitcast.8, f32[1,32]{1,0:T(1,128)} %bitcast.9, f32[1,32]{1,0:T(1,128)} %bitcast.10, ...), custom_call_target="tpu_custom_call" | custom-call | tf_op jit(solution)/shard_map/pallas_call | solution.py:488
  34.9 0.6 %copy.12 = f32[3,4,8,256]{3,2,1,0:T(8,128)} copy(f32[3,4,8,256]{3,2,1,0:T(8,128)S(1)} %shard_map.100) | data formatting | bytes 196608

commit v3 on v2

--- a/solution.py
+++ b/solution.py
@@ -13,6 +13,7 @@
 Y = 8
 X = 256
 R = C * Y
+G = 4
 
 
 def iota(shape, dim):
@@ -44,7 +45,7 @@
     xin, par, w1, w2, fw, raw, ux, edge, ez, halo,
     cols, cols_e, wxy, wxz, wyz, wxy_e, wyz_e, whx, why, bxy, bxz, byz, bxy_e, byz_e, fres,
     hid, hid_e, acc, sm,
-    rz, ys, yr, ds, dr,
+    rel, zs_, zr, rz, ys, yr,
     lsem, ssem, rsem,
 ):
     gz, gy = lax.axis_index("gz"), lax.axis_index("gy")
@@ -53,6 +54,12 @@
     has_y = (gy > 0, gy < ny - 1)
     z_of = (gz - 1, gz + 1)
     y_of = (gy - 1, gy + 1)
+    place = gy % G
+    far = (has_y[0] & (place == 0), has_y[1] & (place == G - 1))
+    way = (gy + G - 1, gy - G + 1)
+    helps = ((place == G - 1) & (gy >= G), (place == 0) & (gy + G < ny))
+    source = (gy - G + 1, gy + G - 1)
+    beyond_group = (gy - G, gy + G)
 
     barrier = pltpu.get_barrier_semaphore()
     for side in range(2):
@@ -63,6 +70,10 @@
         @pl.when(has_y[side])
         def _():
             pl.semaphore_signal(barrier, inc=1, device_id=(gz, y_of[side]), device_id_type=MESH)
+
+        @pl.when(helps[side])
+        def _():
+            pl.semaphore_signal(barrier, inc=1, device_id=(gz, source[side]), device_id_type=MESH)
 
     order = (0, 3, 1, 2)
     loads = {z: pltpu.make_async_copy(x_hbm.at[:, z], xin.at[:, z], lsem.at[z]) for z in order}
@@ -140,15 +151,37 @@
         remote(ux.at[(1, Z)[s], 1], ux.at[(Z + 1, 0)[s], 1], 2 + s, z_of[s], gy) for s in range(2)
     ]
     send_y = [
-        remote(edge.at[:, s], halo.at[pl.ds(1, Z), 1 - s], 4 + s, gz, y_of[s]) for s in range(2)
+        [remote(edge.at[z, s], halo.at[z + 1, 1 - s], 4 + s * Z + z, gz, y_of[s]) for z in range(Z)]
+        for s in range(2)
+    ]
+    send_way = [
+        [remote(edge.at[z, s], rel.at[s, z], 16 + s * (Z - 1) + z, gz, way[s]) for z in range(Z - 1)]
+        for s in range(2)
+    ]
+    pass_on = [
+        [
+            pltpu.make_async_remote_copy(
+                src_ref=rel.at[s, z], dst_ref=halo.at[z + 1, 1 - s], send_sem=ssem.at[28 + s * (Z - 1) + z],
+                recv_sem=rsem.at[4 + s * Z + z], device_id=(gz, beyond_group[s]), device_id_type=MESH,
+            )
+            for z in range(Z - 1)
+        ]
+        for s in range(2)
     ]
     send_corner = [
         [
-            remote(ez.at[zs, ys_], halo.at[(0, Z + 1)[zs], 1 - ys_], 6 + 2 * zs + ys_, gz, y_of[ys_])
+            remote(ez.at[zs, ys_], halo.at[(0, Z + 1)[zs], 1 - ys_], 12 + 2 * zs + ys_, gz, y_of[ys_])
             for ys_ in range(2)
         ]
         for zs in range(2)
     ]
+
+    def relay(s):
+        @pl.when(helps[s])
+        def _():
+            for z in range(Z - 1):
+                send_way[s][z].wait_recv()
+                pass_on[s][z].start()
 
     for copy in weights:
         copy.wait()
@@ -227,7 +260,7 @@
     fres[...] = jnp.where(own, dot(fw16.astype(BF16), spread), 0.0).astype(BF16)
     bias = jnp.sum(fw16 * b2_row, axis=1, keepdims=True)
 
-    peers = sum(flag.astype(jnp.int32) for flag in (*has_z, *has_y))
+    peers = sum(flag.astype(jnp.int32) for flag in (*has_z, *has_y, *far))
     pl.semaphore_wait(barrier, peers)
 
     for side in range(2):
@@ -235,9 +268,16 @@
         def _():
             send_ez[side].start()
     for side in range(2):
-        @pl.when(has_y[side])
-        def _():
-            send_y[side].start()
+        @pl.when(far[side])
+        def _():
+            for z in range(Z - 1):
+                send_way[side][z].start()
+            send_y[side][Z - 1].start()
+
+        @pl.when(has_y[side] & jnp.logical_not(far[side]))
+        def _():
+            for z in range(Z):
+                send_y[side][z].start()
     for side in range(2):
         @pl.when(has_z[side])
         def _():
@@ -288,6 +328,8 @@
                 @pl.when(has_y[yside])
                 def _():
                     send_corner[side][yside].start()
+
+    relay(0)
 
     for z in range(Z):
         xz = dot(wxz[1], ux[z + 1].reshape(3 * R, X))
@@ -320,6 +362,8 @@
     for z in range(1, Z - 1):
         finish(z)
 
+    relay(1)
+
     for side in range(2):
         @pl.when(has_z[side])
         def _():
@@ -335,12 +379,17 @@
     for side in range(2):
         @pl.when(has_y[side])
         def _():
-            send_y[1 - side].wait_recv()
+            for z in range(Z):
+                send_y[1 - side][z].wait_recv()
+    hidden = []
     for z in range(Z):
         beside = halo[z + 1].reshape(2 * C, X)
         wider = beside.astype(F32)
         three = jnp.concatenate([from_left(wider).astype(BF16), beside, from_right(wider).astype(BF16)], axis=0)
-        add_xy(z, dot(bxy_e[...], active_e(hid_e[0, z] + dot(whx[...], three))))
+        hidden.append(hid_e[0, z] + dot(whx[...], three))
+    both = [dot(bxy_e[...], active_e(value)) for value in hidden]
+    for z in range(Z):
+        add_xy(z, both[z])
     for side in range(2):
         @pl.when(has_y[side])
         def _():
@@ -348,9 +397,10 @@
                 @pl.when(has_z[zside])
                 def _():
                     send_corner[zside][1 - side].wait_recv()
+    hidden = [hid_e[1, z] + dot(why[...], halo[z : z + 3].reshape(6 * C, X)) for z in range(Z)]
+    both = [dot(byz_e[...], active_e(value)) for value in hidden]
     for z in range(Z):
-        hidden = hid_e[1, z] + dot(why[...], halo[z : z + 3].reshape(6 * C, X))
-        add_yz(z, dot(byz_e[...], active_e(hidden)))
+        add_yz(z, both[z])
 
     rows16x = iota((16, X), 0)
     outside = ((rows16x == 15) & jnp.logical_not(has_y[0])) | ((rows16x == Y) & jnp.logical_not(has_y[1]))
@@ -379,40 +429,58 @@
             sm[0, zs, comp] = value[:Y]
             sm[1, zs, comp] = value[Y:]
 
-    send_rz = [remote(sm.at[0, pl.ds((0, Z + 2)[t], 2)], rz.at[1 - t], 10 + t, z_of[t], gy) for t in range(2)]
-    send_ry = [remote(ys.at[s], yr.at[1 - s], 12 + s, gz, y_of[s]) for s in range(2)]
-    send_rd = [
-        [remote(ds.at[t, s], dr.at[1 - t, 1 - s], 14 + 2 * t + s, z_of[t], y_of[s]) for s in range(2)]
-        for t in range(2)
-    ]
+    send_zr = [remote(zs_.at[t], zr.at[1 - t], 22 + t, z_of[t], gy) for t in range(2)]
+    send_rz = [remote(sm.at[0, pl.ds((0, Z + 2)[t], 2)], rz.at[1 - t], 24 + t, z_of[t], gy) for t in range(2)]
+    send_ry = [remote(ys.at[s], yr.at[1 - s], 26 + s, gz, y_of[s]) for s in range(2)]
     row = iota((Y, X), 0)
-    sent = (row >= Y - 2, row < 2)
+    low, high = row < 2, row >= Y - 2
 
     def moved(value, by):
         return pltpu.roll(value, by % Y, axis=0) if by % Y else value
 
+    for t in range(2):
+        for comp in range(3):
+            a, b = sm[1, (0, Z + 2)[t], comp], sm[1, (0, Z + 2)[t] + 1, comp]
+            kept = jnp.where(low, a, jnp.where(high, b, 0.0))
+            zs_[t, comp] = kept + moved(jnp.where(high, a, jnp.where(low, b, 0.0)), 4)
+
+        @pl.when(has_z[t])
+        def _():
+            send_zr[t].start()
+
+    for side in range(2):
+        @pl.when(jnp.logical_not(has_z[side]))
+        def _():
+            zr[side] = jnp.zeros((3, Y, X), F32)
+            rz[side] = jnp.zeros((2, 3, Y, X), F32)
+
+        @pl.when(jnp.logical_not(has_y[side]))
+        def _():
+            yr[side] = jnp.zeros((4 * Y, X), BF16)
+
+    for side in range(2):
+        @pl.when(has_z[side])
+        def _():
+            send_zr[1 - side].wait_recv()
+    packs = [[], []]
+    for comp in range(3):
+        up, down = None, None
+        for z in range(Z):
+            value = zr[z // 2, comp]
+            turned = moved(value, 4)
+            if z % 2 == 0:
+                value = jnp.where(low, value, turned)
+            else:
+                value = jnp.where(low, turned, value)
+            value = sm[1, z + 2, comp] + value
+            first = moved(jnp.where(low, value, 0.0), 2 * z)
+            last = moved(jnp.where(high, value, 0.0), 2 * z + 2)
+            up = first if up is None else up + first
+            down = last if down is None else down + last
+        packs[1].append(up)
+        packs[0].append(down)
     for s in range(2):
-        for t in range(2):
-            for tile in range(2):
-                packed = None
-                for comp in range(3):
-                    for q in range(2):
-                        if comp // 2 == tile:
-                            value = jnp.where(sent[s], sm[1, (0, Z + 2)[t] + q, comp], 0.0)
-                            value = moved(value, (comp % 2) * 4 + 2 * q + (2, 0)[s])
-                            packed = value if packed is None else packed + value
-                ds[t, s, tile] = packed
-
-            @pl.when(has_z[t] & has_y[s])
-            def _():
-                send_rd[t][s].start()
-    for s in range(2):
-        for comp in range(3):
-            packed = None
-            for z in range(Z):
-                value = moved(jnp.where(sent[s], sm[1, z + 2, comp], 0.0), 2 * z + (2, 0)[s])
-                packed = value if packed is None else packed + value
-            ys[s, comp] = packed
+        ys[s] = jnp.concatenate([*packs[s], jnp.zeros((Y, X), F32)], axis=0).astype(BF16)
 
         @pl.when(has_y[s])
         def _():
@@ -423,60 +491,55 @@
             send_rz[t].start()
 
     for side in range(2):
-        @pl.when(jnp.logical_not(has_z[side]))
-        def _():
-            rz[side] = jnp.zeros((2, 3, Y, X), F32)
-
-        @pl.when(jnp.logical_not(has_y[side]))
-        def _():
-            yr[side] = jnp.zeros((3, Y, X), F32)
-
-        for s in range(2):
-            @pl.when(jnp.logical_not(has_z[side] & has_y[s]))
-            def _():
-                dr[side, s] = jnp.zeros((2, Y, X), F32)
-
-    for side in range(2):
         @pl.when(has_z[side])
         def _():
             send_rz[1 - side].wait_recv()
-
-        @pl.when(has_y[side])
-        def _():
-            send_ry[1 - side].wait_recv()
-
-        for s in range(2):
-            @pl.when(has_z[side] & has_y[s])
-            def _():
-                send_rd[1 - side][1 - s].wait_recv()
     for comp in range(3):
         for z in range(Z):
-            t, q = z // 2, z % 2
-            beyond = []
-            for s in range(2):
-                to = (0, Y - 2)[s]
-                value = moved(yr[s, comp], to - 2 * z)
-                value += moved(dr[t, s, comp // 2], to - (comp % 2) * 4 - 2 * q)
-                beyond.append(value)
-            value = jnp.where(row < 2, beyond[0], jnp.where(row >= Y - 2, beyond[1], 0.0))
-            out[comp, z] = sm[0, z + 2, comp] + rz[t, q, comp] + value
+            sm[0, z + 2, comp] += rz[z // 2, z % 2, comp]
+    for side in range(2):
+        @pl.when(has_y[side])
+        def _():
+            send_ry[1 - side].wait_recv()
+    came = [yr[s].astype(F32) for s in range(2)]
+    for comp in range(3):
+        for z in range(Z):
+            first = moved(came[0][comp * Y : (comp + 1) * Y], -2 * z)
+            last = moved(came[1][comp * Y : (comp + 1) * Y], -2 - 2 * z)
+            value = jnp.where(low, first, jnp.where(high, last, 0.0))
+            out[comp, z] = sm[0, z + 2, comp] + value
 
     for side in range(2):
         @pl.when(has_z[side])
         def _():
             send_slab[side].wait_send()
+            send_zr[side].wait_send()
             send_rz[side].wait_send()
 
+        @pl.when(far[side])
+        def _():
+            for z in range(Z - 1):
+                send_way[side][z].wait_send()
+            send_y[side][Z - 1].wait_send()
+
+        @pl.when(has_y[side] & jnp.logical_not(far[side]))
+        def _():
+            for z in range(Z):
+                send_y[side][z].wait_send()
+
+        @pl.when(helps[side])
+        def _():
+            for z in range(Z - 1):
+                pass_on[side][z].wait_send()
+
         @pl.when(has_y[side])
         def _():
-            send_y[side].wait_send()
             send_ry[side].wait_send()
 
         for s in range(2):
             @pl.when(has_z[side] & has_y[s])
             def _():
                 send_corner[side][s].wait_send()
-                send_rd[side][s].wait_send()
 
 
 def block(features, s1, t1, w1, b1, s2, t2, w2, b2, fw):
@@ -520,14 +583,15 @@
             vm((2, Z, 2 * C, X), F32),
             vm((3, Z + 2, 3, 2, Y, X), F32),
             vm((2, Z + 4, 3, Y, X), F32),
-            vm((2, 2, 3, Y, X), F32),
+            vm((2, Z - 1, C, X), BF16),
             vm((2, 3, Y, X), F32),
             vm((2, 3, Y, X), F32),
-            vm((2, 2, 2, Y, X), F32),
-            vm((2, 2, 2, Y, X), F32),
+            vm((2, 2, 3, Y, X), F32),
+            vm((2, 4 * Y, X), BF16),
+            vm((2, 4 * Y, X), BF16),
             dma((Z + 9,)),
-            dma((18,)),
-            dma((18,)),
+            dma((34,)),
+            dma((34,)),
         ],
         compiler_params=pltpu.CompilerParams(
             collective_id=0, has_side_effects=True, vmem_limit_bytes=48 * 1024 * 1024

time: 35.7 us -> 33.5 us (0.938)
  the two profiles are of different devices: /device:TPU:158 before, /device:TPU:30 now
where the time goes in v3:
time: 33.5 us; the launch traced here: 33.4 us
  Pallas kernels  32.8 us (98%)
  local copies, waits for them, and re-layouts  0.64 us (2%)
    pallas_call x1, Pallas kernels, block(): pl.pallas_call(kernel, out_shape=pltpu.VMEM((3, Z, Y, X), F32), in_specs=...  32.8 us

profile of v3, /device:TPU:30, one launch (start us, length us, event | category | flops | bytes accessed | tf_op | source)
XLA Modules:
  0.0 33.4 jit_solution(15206638466971634081)
XLA Ops:
  0.0 32.8 %shard_map.100 = f32[3,4,8,256]{3,2,1,0:T(8,128)S(1)} custom-call(bf16[32,4,8,256]{3,2,1,0:T(8,128)(2,1)} %x_hbm.1, f32[1,32]{1,0:T(1,128)} %bitcast.6, f32[1,32]{1,0:T(1,128)} %bitcast.7, bf16[3,3,32,32]{3,2,1,0:T(8,128)(2,1)} %w1_hbm.1, f32[1,32]{1,0:T(1,128)} %bitcast.8, f32[1,32]{1,0:T(1,128)} %bitcast.9, f32[1,32]{1,0:T(1,128)} %bitcast.10, ...), custom_call_target="tpu_custom_call" | custom-call | tf_op jit(solution)/shard_map/pallas_call | solution.py:551
  32.8 0.6 %copy.12 = f32[3,4,8,256]{3,2,1,0:T(8,128)} copy(f32[3,4,8,256]{3,2,1,0:T(8,128)S(1)} %shard_map.100) | data formatting | bytes 196608

commit v4 on v3

--- a/solution.py
+++ b/solution.py
@@ -13,6 +13,7 @@
 Y = 8
 X = 256
 R = C * Y
+K = 2
 G = 4
 
 
@@ -155,7 +156,7 @@
         for s in range(2)
     ]
     send_way = [
-        [remote(edge.at[z, s], rel.at[s, z], 16 + s * (Z - 1) + z, gz, way[s]) for z in range(Z - 1)]
+        [remote(edge.at[z, s], rel.at[s, z], 16 + s * (Z - 1) + z, gz, way[s]) for z in range(K)]
         for s in range(2)
     ]
     pass_on = [
@@ -164,7 +165,7 @@
                 src_ref=rel.at[s, z], dst_ref=halo.at[z + 1, 1 - s], send_sem=ssem.at[28 + s * (Z - 1) + z],
                 recv_sem=rsem.at[4 + s * Z + z], device_id=(gz, beyond_group[s]), device_id_type=MESH,
             )
-            for z in range(Z - 1)
+            for z in range(K)
         ]
         for s in range(2)
     ]
@@ -179,7 +180,7 @@
     def relay(s):
         @pl.when(helps[s])
         def _():
-            for z in range(Z - 1):
+            for z in range(K):
                 send_way[s][z].wait_recv()
                 pass_on[s][z].start()
 
@@ -270,9 +271,10 @@
     for side in range(2):
         @pl.when(far[side])
         def _():
-            for z in range(Z - 1):
+            for z in range(K):
                 send_way[side][z].start()
-            send_y[side][Z - 1].start()
+            for z in range(K, Z):
+                send_y[side][z].start()
 
         @pl.when(has_y[side] & jnp.logical_not(far[side]))
         def _():
@@ -313,6 +315,7 @@
             acc[1, z + 2 - i, 1] += part[i, 1]
 
     acc[...] = jnp.zeros_like(acc)
+    relay(0)
     for z in range(Z):
         wide_x = ux[z + 1].reshape(3 * R, X)
         hid_e[0, z] = dot(wxy_e[...], wide_x)
@@ -328,8 +331,6 @@
                 @pl.when(has_y[yside])
                 def _():
                     send_corner[side][yside].start()
-
-    relay(0)
 
     for z in range(Z):
         xz = dot(wxz[1], ux[z + 1].reshape(3 * R, X))
@@ -518,9 +519,10 @@
 
         @pl.when(far[side])
         def _():
-            for z in range(Z - 1):
+            for z in range(K):
                 send_way[side][z].wait_send()
-            send_y[side][Z - 1].wait_send()
+            for z in range(K, Z):
+                send_y[side][z].wait_send()
 
         @pl.when(has_y[side] & jnp.logical_not(far[side]))
         def _():
@@ -529,7 +531,7 @@
 
         @pl.when(helps[side])
         def _():
-            for z in range(Z - 1):
+            for z in range(K):
                 pass_on[side][z].wait_send()
 
         @pl.when(has_y[side])

time: 33.5 us -> 30.7 us (0.916)
  the two profiles are of different devices: /device:TPU:30 before, /device:TPU:386 now
where the time goes in v4:
time: 30.7 us; the launch traced here: 30.6 us
  Pallas kernels  29.9 us (97%)
  local copies, waits for them, and re-layouts  0.64 us (2%)
    pallas_call x1, Pallas kernels, block(): pl.pallas_call(kernel, out_shape=pltpu.VMEM((3, Z, Y, X), F32), in_specs=...  29.9 us
    unnamed x1, local copies, waits for them, and re-layouts  0.64 us

profile of v4, /device:TPU:386, one launch (start us, length us, event | category | flops | bytes accessed | tf_op | source)
XLA Modules:
  0.0 30.6 jit_solution(10943117044244729767)
XLA Ops:
  0.0 29.9 %shard_map.100 = f32[3,4,8,256]{3,2,1,0:T(8,128)S(1)} custom-call(bf16[32,4,8,256]{3,2,1,0:T(8,128)(2,1)} %x_hbm.1, f32[1,32]{1,0:T(1,128)} %bitcast.6, f32[1,32]{1,0:T(1,128)} %bitcast.7, bf16[3,3,32,32]{3,2,1,0:T(8,128)(2,1)} %w1_hbm.1, f32[1,32]{1,0:T(1,128)} %bitcast.8, f32[1,32]{1,0:T(1,128)} %bitcast.9, f32[1,32]{1,0:T(1,128)} %bitcast.10, ...), custom_call_target="tpu_custom_call" | custom-call | tf_op jit(solution)/shard_map/pallas_call | solution.py:553
  29.9 0.6 %copy.12 = f32[3,4,8,256]{3,2,1,0:T(8,128)} copy(f32[3,4,8,256]{3,2,1,0:T(8,128)S(1)} %shard_map.100) | data formatting | bytes 196608

commit v5 on v4

--- a/solution.py
+++ b/solution.py
@@ -13,7 +13,8 @@
 Y = 8
 X = 256
 R = C * Y
-K = 2
+K = 3
+NEAR = 2
 G = 4
 
 
@@ -61,6 +62,9 @@
     helps = ((place == G - 1) & (gy >= G), (place == 0) & (gy + G < ny))
     source = (gy - G + 1, gy + G - 1)
     beyond_group = (gy - G, gy + G)
+    near_way = (gy + 1, gy - 1)
+    near_helps = ((place == 1) & (gy >= G), (place == G - 2) & (gy + 2 < ny))
+    near_beyond = (gy - 2, gy + 2)
 
     barrier = pltpu.get_barrier_semaphore()
     for side in range(2):
@@ -156,14 +160,14 @@
         for s in range(2)
     ]
     send_way = [
-        [remote(edge.at[z, s], rel.at[s, z], 16 + s * (Z - 1) + z, gz, way[s]) for z in range(K)]
+        [remote(edge.at[z, s], rel.at[s, z], 16 + s * (Z - 1) + z, gz, (way if z < NEAR else near_way)[s]) for z in range(K)]
         for s in range(2)
     ]
     pass_on = [
         [
             pltpu.make_async_remote_copy(
                 src_ref=rel.at[s, z], dst_ref=halo.at[z + 1, 1 - s], send_sem=ssem.at[28 + s * (Z - 1) + z],
-                recv_sem=rsem.at[4 + s * Z + z], device_id=(gz, beyond_group[s]), device_id_type=MESH,
+                recv_sem=rsem.at[4 + s * Z + z], device_id=(gz, (beyond_group if z < NEAR else near_beyond)[s]), device_id_type=MESH,
             )
             for z in range(K)
         ]
@@ -178,11 +182,12 @@
     ]
 
     def relay(s):
-        @pl.when(helps[s])
-        def _():
-            for z in range(K):
-                send_way[s][z].wait_recv()
-                pass_on[s][z].start()
+        for flag, rows in ((helps[s], range(NEAR)), (near_helps[s], range(NEAR, K))):
+            @pl.when(flag)
+            def _():
+                for z in rows:
+                    send_way[s][z].wait_recv()
+                    pass_on[s][z].start()
 
     for copy in weights:
         copy.wait()
@@ -529,10 +534,11 @@
             for z in range(Z):
                 send_y[side][z].wait_send()
 
-        @pl.when(helps[side])
-        def _():
-            for z in range(K):
-                pass_on[side][z].wait_send()
+        for flag, rows in ((helps[side], range(NEAR)), (near_helps[side], range(NEAR, K))):
+            @pl.when(flag)
+            def _():
+                for z in rows:
+                    pass_on[side][z].wait_send()
 
         @pl.when(has_y[side])
         def _():

time: 30.7 us -> 30.1 us (0.980)
  the two profiles are of different devices: /device:TPU:386 before, /device:TPU:19 now
where the time goes in v5:
time: 30.1 us; the launch traced here: 30 us
  Pallas kernels  29.3 us (97%)
  local copies, waits for them, and re-layouts  0.64 us (2%)
    pallas_call x1, Pallas kernels, block(): pl.pallas_call(kernel, out_shape=pltpu.VMEM((3, Z, Y, X), F32), in_specs=...  29.3 us
    unnamed x1, local copies, waits for them, and re-layouts  0.64 us

profile of v5, /device:TPU:19, one launch (start us, length us, event | category | flops | bytes accessed | tf_op | source)
XLA Modules:
  0.0 30.0 jit_solution(10755901952820178519)
XLA Ops:
  0.0 29.3 %shard_map.100 = f32[3,4,8,256]{3,2,1,0:T(8,128)S(1)} custom-call(bf16[32,4,8,256]{3,2,1,0:T(8,128)(2,1)} %x_hbm.1, f32[1,32]{1,0:T(1,128)} %bitcast.6, f32[1,32]{1,0:T(1,128)} %bitcast.7, bf16[3,3,32,32]{3,2,1,0:T(8,128)(2,1)} %w1_hbm.1, f32[1,32]{1,0:T(1,128)} %bitcast.8, f32[1,32]{1,0:T(1,128)} %bitcast.9, f32[1,32]{1,0:T(1,128)} %bitcast.10, ...), custom_call_target="tpu_custom_call" | custom-call | tf_op jit(solution)/shard_map/pallas_call | solution.py:559
  29.3 0.6 %copy.12 = f32[3,4,8,256]{3,2,1,0:T(8,128)} copy(f32[3,4,8,256]{3,2,1,0:T(8,128)S(1)} %shard_map.100) | data formatting | bytes 196608

commit v6 on v5

--- a/solution.py
+++ b/solution.py
@@ -276,7 +276,7 @@
     for side in range(2):
         @pl.when(far[side])
         def _():
-            for z in range(K):
+            for z in (*range(NEAR, K), *range(NEAR)):
                 send_way[side][z].start()
             for z in range(K, Z):
                 send_y[side][z].start()
@@ -336,6 +336,8 @@
                 @pl.when(has_y[yside])
                 def _():
                     send_corner[side][yside].start()
+
+    relay(1)
 
     for z in range(Z):
         xz = dot(wxz[1], ux[z + 1].reshape(3 * R, X))
@@ -367,8 +369,6 @@
 
     for z in range(1, Z - 1):
         finish(z)
-
-    relay(1)
 
     for side in range(2):
         @pl.when(has_z[side])

time: 30.1 us -> 30.1 us (level)
  no operation moved by 1% of the time
where the time goes in v6:
time: 30.1 us; the launch traced here: 30 us
  Pallas kernels  29.3 us (97%)
  local copies, waits for them, and re-layouts  0.64 us (2%)
    pallas_call x1, Pallas kernels, block(): pl.pallas_call(kernel, out_shape=pltpu.VMEM((3, Z, Y, X), F32), in_specs=...  29.3 us
    unnamed x1, local copies, waits for them, and re-layouts  0.64 us

profile of v6, /device:TPU:19, one launch (start us, length us, event | category | flops | bytes accessed | tf_op | source)
XLA Modules:
  0.0 30.0 jit_solution(10870573289128761764)
XLA Ops:
  0.0 29.3 %shard_map.100 = f32[3,4,8,256]{3,2,1,0:T(8,128)S(1)} custom-call(bf16[32,4,8,256]{3,2,1,0:T(8,128)(2,1)} %x_hbm.1, f32[1,32]{1,0:T(1,128)} %bitcast.6, f32[1,32]{1,0:T(1,128)} %bitcast.7, bf16[3,3,32,32]{3,2,1,0:T(8,128)(2,1)} %w1_hbm.1, f32[1,32]{1,0:T(1,128)} %bitcast.8, f32[1,32]{1,0:T(1,128)} %bitcast.9, f32[1,32]{1,0:T(1,128)} %bitcast.10, ...), custom_call_target="tpu_custom_call" | custom-call | tf_op jit(solution)/shard_map/pallas_call | solution.py:559
  29.3 0.6 %copy.12 = f32[3,4,8,256]{3,2,1,0:T(8,128)} copy(f32[3,4,8,256]{3,2,1,0:T(8,128)S(1)} %shard_map.100) | data formatting | bytes 196608
